TPU v7x, 32 devices: a whole 2x2x4 slice. The times are simulated.
32 devices in a mesh: section: 2 (over x), dp: 4 (over z), mp: 4 (over y, core).
Axes of the slice: x: 2, y: 2, z: 4, core: 2. Of those that a mesh axis runs over, the one named last changes fastest.
Arguments:
- inputs: bfloat16 [2, 2, 4096, 512], P('section', None, ('dp', 'mp')), may hold values from -6 to 6
- cotangent: bfloat16 [2, 2, 4096, 512], P('section', None, ('dp', 'mp')), may hold values from -6 to 6
- expert_ids: int32 [2, 2, 4096, 1], P('section', None, ('dp', 'mp')), may hold values from 0 to 7; in each aligned block of 256 rows (0 to 255, 256 to 511, ..., all dimensions but the last counted through in order) at most 48 rows name the same one
- self_proj: bfloat16 [2, 512, 8, 256], P('section', None, 'mp')
- cross_proj: bfloat16 [2, 512, 8, 128], P('section', None, 'mp')
- gains: float32 [2, 3, 512], P('section'), may hold values from 0.5 to 1.5
- w_in: bfloat16 [2, 8, 512, 2048], P('section', 'mp'), may hold values from -0.25 to 0.25
- w_out: bfloat16 [2, 8, 2048, 512], P('section', 'mp'), may hold values from -0.1875 to 0.1875
Outputs:
- outputs: bfloat16 [2, 2, 4096, 512], P('section', None, ('dp', 'mp'))
- input_grad: float32 [2, 2, 4096, 512], P('section', None, ('dp', 'mp'))
- self_grad: float32 [2, 512, 8, 256], P('section', None, 'mp')
- cross_grad: float32 [2, 512, 8, 128], P('section', None, 'mp')
- gain_grad: float32 [2, 3, 512], P('section')
- w_in_grad: float32 [2, 8, 512, 2048], P('section', 'mp')
- w_out_grad: float32 [2, 8, 2048, 512], P('section', 'mp')
Inputs may be any that keep to these rules, and one draw needn't show every extreme that they name: `expert_ids`: in the 256 rows of one device in one micro-batch (aligned blocks of the rows of both layers taken in order) no expert is named by more than 48 rows, a bound that some block reaches.
All inputs are finite; a program needn't handle non-finite values.
Results may differ from a plain program's by a relative error of at most 0.023.
Values may be sent and summed in bfloat16 or wider, within the bound.
No kernel may reach another device: no remote copies, remote signals or barrier semaphores. Data moves between devices by JAX's collectives and lax.ppermute only.
A program may use at most 256 MiB of HBM per device.

v0:
```python
import jax
import jax.numpy as jnp
from jax import lax
from jax.sharding import PartitionSpec as P

SEQ = 1024


EPS = 1e-05
NEG = -1000000000.0


def shifted(shard, axis, by):
    count = lax.axis_size(axis)
    pairs = [(i, i + by) for i in range(count) if 0 <= i + by < count]
    return lax.ppermute(shard, axis, pairs)


def norm_rows(residual, gain):
    centre = jnp.mean(residual, axis=-1, keepdims=True)
    centred = residual - centre
    spread = jnp.mean(centred * centred, axis=-1, keepdims=True)
    inverse = lax.rsqrt(spread + EPS)
    normed = centred * inverse
    return (normed * gain, normed, inverse)


def norm_back(upstream, normed, inverse, gain):
    scaled = upstream * gain
    inner = (
        scaled
        - jnp.mean(scaled, axis=-1, keepdims=True)
        - normed * jnp.mean(scaled * normed, axis=-1, keepdims=True)
    )
    return (inverse * inner, jnp.sum(upstream * normed, axis=0))


def softmax_weights(query_rows, key_rows, allowed, scale):
    raw = (
        jnp.einsum("qhe,khe->hqk", query_rows, key_rows, preferred_element_type=jnp.float32) * scale
    )
    scores = jnp.where(allowed[None], raw, NEG)
    peak = jnp.max(scores, axis=-1, keepdims=True)
    powers = jnp.exp(scores - peak)
    return powers / jnp.sum(powers, axis=-1, keepdims=True)


def split_sequences(array, length):
    return array.reshape(array.shape[0] // length, length, array.shape[1], array.shape[2])


def mask_for(causal, length):
    places = jnp.arange(length)
    return jnp.logical_or(places[None, :] <= places[:, None], jnp.logical_not(causal))


def attend_forward(queries, keys, values, causal, length):
    scale = queries.shape[2] ** (-0.5)
    allowed = mask_for(causal, length)

    def one_sequence(parts):
        query_rows, key_rows, value_rows = parts
        weights = softmax_weights(query_rows, key_rows, allowed, scale)
        mixed = jnp.einsum(
            "hqk,khe->qhe",
            weights.astype(jnp.bfloat16),
            value_rows,
            preferred_element_type=jnp.float32,
        )
        return mixed.astype(jnp.bfloat16)

    parts = (
        split_sequences(queries, length),
        split_sequences(keys, length),
        split_sequences(values, length),
    )
    return lax.map(one_sequence, parts).reshape(queries.shape)


def attend_backward(queries, keys, values, out_grad, causal, length):
    scale = queries.shape[2] ** (-0.5)
    allowed = mask_for(causal, length)

    def one_sequence(parts):
        query_rows, key_rows, value_rows, grad_rows = parts
        weights = softmax_weights(query_rows, key_rows, allowed, scale)
        prob_grad = jnp.einsum(
            "qhe,khe->hqk", grad_rows, value_rows, preferred_element_type=jnp.float32
        )
        inner = jnp.sum(prob_grad * weights, axis=-1, keepdims=True)
        score_grad = (weights * (prob_grad - inner)).astype(jnp.bfloat16)
        query_grad = (
            jnp.einsum("hqk,khe->qhe", score_grad, key_rows, preferred_element_type=jnp.float32)
            * scale
        )
        key_grad = (
            jnp.einsum("hqk,qhe->khe", score_grad, query_rows, preferred_element_type=jnp.float32)
            * scale
        )
        value_grad = jnp.einsum(
            "hqk,qhe->khe",
            weights.astype(jnp.bfloat16),
            grad_rows,
            preferred_element_type=jnp.float32,
        )
        return (query_grad, key_grad, value_grad)

    parts = (
        split_sequences(queries, length),
        split_sequences(keys, length),
        split_sequences(values, length),
        split_sequences(out_grad, length),
    )
    results = lax.map(one_sequence, parts)
    return tuple((piece.reshape(queries.shape) for piece in results))


def place_row(store, index, valid, row):
    current = lax.dynamic_index_in_dim(store, index, 0, keepdims=False)
    return lax.dynamic_update_index_in_dim(store, jnp.where(valid, row, current), index, 0)


def on_device(inputs, cotangent, expert_ids, self_proj, cross_proj, gains, w_in, w_out):
    micro = inputs.shape[1]
    tokens = inputs.shape[2]
    width = inputs.shape[3]
    parts = lax.axis_size("mp")
    group = tokens * parts
    local_heads = self_proj.shape[2]
    head_size = self_proj.shape[3] // 4
    local_experts = w_in.shape[1]
    experts = local_experts * parts
    capacity = max(2, 3 * tokens // (2 * experts))
    length = SEQ
    section_index = lax.axis_index("section")
    decoder = section_index == 1
    triple_weight = self_proj[0][:, :, : 3 * head_size]
    exit_weight = self_proj[0][:, :, 3 * head_size :]
    cross_weight = cross_proj[0]
    query_weight = cross_weight[:, :, :head_size]
    cross_exit = cross_weight[:, :, head_size:]
    gain_set = gains[0]
    first_weight = w_in[0]
    second_weight = w_out[0]
    no_mask = jnp.asarray(False)

    def collect(piece):
        return lax.all_gather(piece, "mp", axis=0, tiled=True)

    def spread(partial_sum):
        return lax.psum_scatter(
            partial_sum.astype(jnp.bfloat16), "mp", scatter_dimension=0, tiled=True
        ).astype(jnp.float32)

    def route(buffer):
        return lax.all_to_all(buffer, "mp", split_axis=0, concat_axis=0, tiled=True)

    def step_index(step):
        index = step - 2 * section_index
        valid = jnp.logical_and(index >= 0, index < micro)
        return (valid, jnp.clip(index, 0, micro - 1))

    def forward_step(step, memory_prev, keys_in):
        valid, clamped = step_index(step)
        residual = lax.dynamic_index_in_dim(inputs[0], clamped, 0, keepdims=False).astype(
            jnp.float32
        )
        labels = lax.dynamic_index_in_dim(expert_ids[0], clamped, 0, keepdims=False)[:, 0]
        normed_a, unit_a, inverse_a = norm_rows(residual, gain_set[0])
        rows_a = collect(normed_a.astype(jnp.bfloat16))
        projected = jnp.einsum(
            "td,dhf->thf", rows_a, triple_weight, preferred_element_type=jnp.float32
        ).astype(jnp.bfloat16)
        queries = projected[:, :, :head_size]
        keys = projected[:, :, head_size : 2 * head_size]
        values = projected[:, :, 2 * head_size :]
        heads = attend_forward(queries, keys, values, decoder, length)
        attended = spread(
            jnp.einsum("the,dhe->td", heads, exit_weight, preferred_element_type=jnp.float32)
        )
        after_self = residual + attended
        slot_source = jnp.where(decoder, after_self, memory_prev)
        normed_c, unit_c, inverse_c = norm_rows(slot_source, gain_set[1])
        rows_c = collect(normed_c.astype(jnp.bfloat16))

        def encoder_slot(operands):
            made = jnp.einsum(
                "td,dhf->thf", operands[0], cross_weight, preferred_element_type=jnp.float32
            ).astype(jnp.bfloat16)
            blank = jnp.zeros((group, local_heads, head_size), jnp.bfloat16)
            return (made, jnp.zeros((group, width), jnp.float32), blank, blank)

        def decoder_slot(operands):
            received = operands[1]
            cross_queries = jnp.einsum(
                "td,dhe->the", operands[0], query_weight, preferred_element_type=jnp.float32
            ).astype(jnp.bfloat16)
            cross_heads = attend_forward(
                cross_queries,
                received[:, :, :head_size],
                received[:, :, head_size:],
                no_mask,
                length,
            )
            partial_sum = jnp.einsum(
                "the,dhe->td", cross_heads, cross_exit, preferred_element_type=jnp.float32
            )
            return (jnp.zeros_like(received), partial_sum, cross_queries, cross_heads)

        keys_out, cross_part, cross_queries, cross_heads = lax.cond(
            decoder, decoder_slot, encoder_slot, (rows_c, keys_in)
        )
        after_cross = after_self + spread(cross_part)
        normed_f, unit_f, inverse_f = norm_rows(after_cross, gain_set[2])
        chosen = normed_f.astype(jnp.bfloat16)
        hot = (labels[:, None] == jnp.arange(experts)[None, :]).astype(jnp.int32)
        slot = jnp.sum((jnp.cumsum(hot, axis=0) - hot) * hot, axis=1)
        place = labels * capacity + slot
        sources = (
            jnp.full((experts * capacity,), tokens, jnp.int32)
            .at[place]
            .set(jnp.arange(tokens, dtype=jnp.int32))
        )
        padded = jnp.concatenate([chosen, jnp.zeros((1, width), jnp.bfloat16)], axis=0)
        incoming = route(padded[sources].reshape(parts, local_experts, capacity, width))
        before = jnp.einsum(
            "secd,edf->secf", incoming, first_weight, preferred_element_type=jnp.float32
        )
        hidden = jax.nn.gelu(before).astype(jnp.bfloat16)
        produced = jnp.einsum(
            "secf,efd->secd", hidden, second_weight, preferred_element_type=jnp.float32
        ).astype(jnp.bfloat16)
        returned = route(produced).reshape(experts * capacity, width)
        output = after_cross + returned[place].astype(jnp.float32)
        kept = {
            "unit_a": unit_a,
            "inverse_a": inverse_a,
            "rows_a": rows_a,
            "queries": queries,
            "keys": keys,
            "values": values,
            "heads": heads,
            "own_heads": heads,
            "unit_c": unit_c,
            "inverse_c": inverse_c,
            "rows_c": rows_c,
            "cross_queries": cross_queries,
            "cross_heads": cross_heads,
            "unit_f": unit_f,
            "inverse_f": inverse_f,
            "sources": sources,
            "place": place,
            "incoming": incoming,
            "before": before,
            "hidden": hidden,
        }
        return (output, keys_out, kept)

    steps = micro + 2
    memory_prev = jnp.zeros((tokens, width), jnp.float32)
    keys_in = jnp.zeros((group, local_heads, 2 * head_size), jnp.bfloat16)
    outputs = jnp.zeros((micro, tokens, width), jnp.float32)
    kept_memory = []
    kept_keys = []
    for step in range(steps):
        kept_memory.append(memory_prev)
        kept_keys.append(keys_in)
        valid, clamped = step_index(step)
        output, keys_out, kept = forward_step(step, memory_prev, keys_in)
        outputs = place_row(outputs, clamped, valid, output)
        memory_prev = output
        if step + 1 < steps:
            keys_in = shifted(keys_out, "section", 1)
    carry = jnp.zeros((tokens, width), jnp.float32)
    keys_grad_in = jnp.zeros((group, local_heads, 2 * head_size), jnp.bfloat16)
    input_grads = jnp.zeros((micro, tokens, width), jnp.float32)
    triple_total = jnp.zeros(triple_weight.shape, jnp.float32)
    exit_total = jnp.zeros(exit_weight.shape, jnp.float32)
    cross_total = jnp.zeros(cross_weight.shape, jnp.float32)
    first_total = jnp.zeros(first_weight.shape, jnp.float32)
    second_total = jnp.zeros(second_weight.shape, jnp.float32)
    gain_total = jnp.zeros(gain_set.shape, jnp.float32)
    for step in reversed(range(steps)):
        valid, clamped = step_index(step)
        slot_valid = jnp.where(decoder, valid, jnp.logical_and(step >= 1, step <= micro))
        out_grad = (
            lax.dynamic_index_in_dim(cotangent[0], clamped, 0, keepdims=False).astype(jnp.float32)
            + carry
        )
        backward_memory_prev = kept_memory[step]
        backward_keys_in = kept_keys[step]
        backward_output, backward_keys_out, backward_kept = forward_step(
            step, backward_memory_prev, backward_keys_in
        )
        back_rows = out_grad.astype(jnp.bfloat16)
        padded_back = jnp.concatenate([back_rows, jnp.zeros((1, width), jnp.bfloat16)], axis=0)
        incoming_back = route(
            padded_back[backward_kept["sources"]].reshape(parts, local_experts, capacity, width)
        )
        hidden_grad = jnp.einsum(
            "secd,efd->secf", incoming_back, second_weight, preferred_element_type=jnp.float32
        )
        second_grad = jnp.einsum(
            "secf,secd->efd",
            backward_kept["hidden"],
            incoming_back,
            preferred_element_type=jnp.float32,
        )
        gelu_pull = jax.vjp(jax.nn.gelu, backward_kept["before"])[1]
        before_grad = gelu_pull(hidden_grad)[0].astype(jnp.bfloat16)
        first_grad = jnp.einsum(
            "secd,secf->edf",
            backward_kept["incoming"],
            before_grad,
            preferred_element_type=jnp.float32,
        )
        slot_rows = jnp.einsum(
            "secf,edf->secd", before_grad, first_weight, preferred_element_type=jnp.float32
        ).astype(jnp.bfloat16)
        chosen_grad = (
            route(slot_rows)
            .reshape(experts * capacity, width)[backward_kept["place"]]
            .astype(jnp.float32)
        )
        norm_grad_f, gain_f = norm_back(
            chosen_grad, backward_kept["unit_f"], backward_kept["inverse_f"], gain_set[2]
        )
        cross_out_grad = out_grad + norm_grad_f
        rows_grad_c = collect(cross_out_grad.astype(jnp.bfloat16))

        def decoder_back(operands):
            rows_grad = operands[0]
            heads_grad = jnp.einsum(
                "td,dhe->the", rows_grad, cross_exit, preferred_element_type=jnp.float32
            ).astype(jnp.bfloat16)
            exit_grad = jnp.einsum(
                "td,the->dhe",
                rows_grad,
                backward_kept["cross_heads"],
                preferred_element_type=jnp.float32,
            )
            query_grad, key_grad, value_grad = attend_backward(
                backward_kept["cross_queries"],
                backward_keys_in[:, :, :head_size],
                backward_keys_in[:, :, head_size:],
                heads_grad,
                no_mask,
                length,
            )
            query_low = query_grad.astype(jnp.bfloat16)
            near_grad = jnp.einsum(
                "td,the->dhe",
                backward_kept["rows_c"],
                query_low,
                preferred_element_type=jnp.float32,
            )
            rows_back = jnp.einsum(
                "the,dhe->td", query_low, query_weight, preferred_element_type=jnp.float32
            )
            sent = jnp.concatenate([key_grad, value_grad], axis=2).astype(jnp.bfloat16)
            return (rows_back, jnp.concatenate([near_grad, exit_grad], axis=2), sent)

        def encoder_back(operands):
            weight_grad = jnp.einsum(
                "td,thf->dhf",
                backward_kept["rows_c"],
                keys_grad_in,
                preferred_element_type=jnp.float32,
            )
            rows_back = jnp.einsum(
                "thf,dhf->td", keys_grad_in, cross_weight, preferred_element_type=jnp.float32
            )
            return (rows_back, weight_grad, jnp.zeros_like(keys_grad_in))

        rows_back_c, slot_grad, sent = lax.cond(decoder, decoder_back, encoder_back, (rows_grad_c,))
        summed_c = spread(rows_back_c)
        source_grad, gain_c = norm_back(
            summed_c, backward_kept["unit_c"], backward_kept["inverse_c"], gain_set[1]
        )
        self_out_grad = cross_out_grad + jnp.where(decoder, source_grad, 0.0)
        memory_grad = jnp.where(decoder, 0.0, source_grad)
        low_grad = self_out_grad.astype(jnp.bfloat16)
        rows_grad_a = collect(low_grad)
        heads_grad = jnp.einsum(
            "td,dhe->the", rows_grad_a, exit_weight, preferred_element_type=jnp.float32
        ).astype(jnp.bfloat16)
        exit_grad = jnp.einsum(
            "td,the->dhe", rows_grad_a, backward_kept["heads"], preferred_element_type=jnp.float32
        )
        query_grad, key_grad, value_grad = attend_backward(
            backward_kept["queries"],
            backward_kept["keys"],
            backward_kept["values"],
            heads_grad,
            decoder,
            length,
        )
        triple_low = jnp.concatenate([query_grad, key_grad, value_grad], axis=2).astype(
            jnp.bfloat16
        )
        triple_grad = jnp.einsum(
            "td,thf->dhf", backward_kept["rows_a"], triple_low, preferred_element_type=jnp.float32
        )
        summed_a = spread(
            jnp.einsum("thf,dhf->td", triple_low, triple_weight, preferred_element_type=jnp.float32)
        )
        norm_grad_a, gain_a = norm_back(
            summed_a, backward_kept["unit_a"], backward_kept["inverse_a"], gain_set[0]
        )
        input_grad = self_out_grad + norm_grad_a
        input_grad, memory_grad, sent, pieces = (
            input_grad,
            memory_grad,
            sent,
            (triple_grad, exit_grad, slot_grad, first_grad, second_grad, gain_a, gain_c, gain_f),
        )
        triple_grad, exit_grad, slot_grad, first_grad, second_grad, gain_a, gain_c, gain_f = pieces
        carry = jnp.where(slot_valid, memory_grad, 0.0)
        if step > 0:
            keys_grad_in = shifted(sent, "section", -1)
        input_grads = place_row(input_grads, clamped, valid, input_grad)
        triple_total = triple_total + jnp.where(valid, triple_grad, 0.0)
        exit_total = exit_total + jnp.where(valid, exit_grad, 0.0)
        cross_total = cross_total + jnp.where(slot_valid, slot_grad, 0.0)
        first_total = first_total + jnp.where(valid, first_grad, 0.0)
        second_total = second_total + jnp.where(valid, second_grad, 0.0)
        gain_step = jnp.stack(
            [
                jnp.where(valid, gain_a, 0.0),
                jnp.where(slot_valid, gain_c, 0.0),
                jnp.where(valid, gain_f, 0.0),
            ]
        )
        gain_total = gain_total + gain_step
    self_total = jnp.concatenate([triple_total, exit_total], axis=2)
    self_total, cross_total, first_total, second_total = (
        lax.psum(self_total.astype(jnp.bfloat16), "dp").astype(jnp.float32),
        lax.psum(cross_total.astype(jnp.bfloat16), "dp").astype(jnp.float32),
        lax.psum(first_total.astype(jnp.bfloat16), "dp").astype(jnp.float32),
        lax.psum(second_total.astype(jnp.bfloat16), "dp").astype(jnp.float32),
    )
    gain_total = lax.psum(gain_total, ("dp", "mp"))
    return (
        outputs.astype(jnp.bfloat16)[None],
        input_grads[None],
        self_total[None],
        cross_total[None],
        gain_total[None],
        first_total[None],
        second_total[None],
    )


def solution(mesh):
    return jax.shard_map(
        on_device,
        mesh=mesh,
        in_specs=(
            P("section", None, ("dp", "mp"), None),
            P("section", None, ("dp", "mp"), None),
            P("section", None, ("dp", "mp"), None),
            P("section", None, "mp", None),
            P("section", None, "mp", None),
            P("section", None, None),
            P("section", "mp", None, None),
            P("section", "mp", None, None),
        ),
        out_specs=(
            P("section", None, ("dp", "mp"), None),
            P("section", None, ("dp", "mp"), None),
            P("section", None, "mp", None),
            P("section", None, "mp", None),
            P("section", None, None),
            P("section", "mp", None, None),
            P("section", "mp", None, None),
        ),
        check_vma=False,
    )
```

profile of v0, /device:TPU:0, one launch (start us, length us, event | category | flops | bytes accessed | tf_op | source)
XLA Modules:
  0.0 1532.9 jit_solution(2449894957559920136)
XLA Ops:
  14.8 17.8 %all-gather.17.cloned.1.call-done = bf16[1024,512]{1,0:T(8,128)(2,1)} async-done(((bf16[256,512]{1,0:T(8,128)(2,1)}), bf16[1024,512]{1,0:T(8,128)(2,1)}) %all-gather.17.cloned.1.call-update) | async-done | bytes 1048592 | tf_op jit(solution)/shard_map/all_gather | solution.py:148
  45.6 24.9 %reduce-scatter.21.cloned.1.call-done = bf16[256,512]{1,0:T(8,128)(2,1)} async-done(((bf16[1024,512]{1,0:T(8,128)(2,1)}), bf16[256,512]{1,0:T(8,128)(2,1)}) %reduce-scatter.21.cloned.1.call-update) | async-done | bytes 262160 | tf_op jit(solution)/shard_map/reduce_scatter | solution.py:151
  75.3 16.6 %all-gather.19.cloned.1.call-done = bf16[1024,512]{1,0:T(8,128)(2,1)} async-done(((bf16[256,512]{1,0:T(8,128)(2,1)}), bf16[1024,512]{1,0:T(8,128)(2,1)}) %all-gather.19.cloned.1.call-update) | async-done | bytes 1048592 | tf_op jit(solution)/shard_map/all_gather | solution.py:148
  98.3 32.8 %reduce-scatter.55.cloned.1.call-done = bf16[256,512]{1,0:T(8,128)(2,1)} async-done(((bf16[1024,512]{1,0:T(8,128)(2,1)}), bf16[256,512]{1,0:T(8,128)(2,1)}) %reduce-scatter.55.cloned.1.call-update) | async-done | bytes 262160 | tf_op jit(solution)/shard_map/reduce_scatter | solution.py:151
  131.1 27.9 %reduce-scatter.23.cloned.1.call-done = bf16[256,512]{1,0:T(8,128)(2,1)} async-done(((bf16[1024,512]{1,0:T(8,128)(2,1)}), bf16[256,512]{1,0:T(8,128)(2,1)}) %reduce-scatter.23.cloned.1.call-update) | async-done | bytes 262160 | tf_op jit(solution)/shard_map/reduce_scatter | solution.py:151
  165.9 12.9 all-gather.21.cloned.1.call-done
  181.7 8.1 fusion.1080
  198.5 11.1 all_to_all.100
  209.6 6.3 fusion.567
  221.3 7.3 all-to-all-done.1
  239.0 11.3 collective-permute-done
  259.7 8.3 all-gather.25.cloned.1.call-done
  270.9 7.9 fusion.1089
  284.8 11.1 reduce-scatter.49.cloned.1.call-done
  295.9 28.2 %reduce-scatter.27.cloned.1.call-done = bf16[256,512]{1,0:T(8,128)(2,1)} async-done(((bf16[1024,512]{1,0:T(8,128)(2,1)}), bf16[256,512]{1,0:T(8,128)(2,1)}) %reduce-scatter.27.cloned.1.call-update) | async-done | bytes 262160 | tf_op jit(solution)/shard_map/reduce_scatter | solution.py:151
  329.9 10.0 all_to_all.101
  349.8 7.3 all-to-all-done.3
  366.5 11.3 collective-permute-done.1
  397.6 7.0 fusion.1098
  410.7 13.0 reduce-scatter.43.cloned.1.call-done
  423.7 27.9 %reduce-scatter.31.cloned.1.call-done = bf16[256,512]{1,0:T(8,128)(2,1)} async-done(((bf16[1024,512]{1,0:T(8,128)(2,1)}), bf16[256,512]{1,0:T(8,128)(2,1)}) %reduce-scatter.31.cloned.1.call-update) | async-done | bytes 262160 | tf_op jit(solution)/shard_map/reduce_scatter | solution.py:151
  456.3 9.8 all_to_all.102
  476.4 6.9 all-to-all-done.5
  492.3 10.2 collective-permute-done.2
  508.7 36.3 %reduce-scatter.37.cloned.1.call-done = bf16[256,512]{1,0:T(8,128)(2,1)} async-done(((bf16[1024,512]{1,0:T(8,128)(2,1)}), bf16[256,512]{1,0:T(8,128)(2,1)}) %reduce-scatter.37.cloned.1.call-update) | async-done | bytes 262160 | tf_op jit(solution)/shard_map/reduce_scatter | solution.py:151
  545.0 28.0 %reduce-scatter.35.cloned.1.call-done = bf16[256,512]{1,0:T(8,128)(2,1)} async-done(((bf16[1024,512]{1,0:T(8,128)(2,1)}), bf16[256,512]{1,0:T(8,128)(2,1)}) %reduce-scatter.35.cloned.1.call-update) | async-done | bytes 262160 | tf_op jit(solution)/shard_map/reduce_scatter | solution.py:151
  625.0 16.8 %all-gather.33.cloned.1.call-done = bf16[1024,512]{1,0:T(8,128)(2,1)} async-done(((bf16[256,512]{1,0:T(8,128)(2,1)}), bf16[1024,512]{1,0:T(8,128)(2,1)}) %all-gather.33.cloned.1.call-update) | async-done | bytes 1048592 | tf_op jit(solution)/shard_map/all_gather | solution.py:148
  654.6 38.2 %reduce-scatter.39.cloned.1.call-done = bf16[256,512]{1,0:T(8,128)(2,1)} async-done(((bf16[1024,512]{1,0:T(8,128)(2,1)}), bf16[256,512]{1,0:T(8,128)(2,1)}) %reduce-scatter.39.cloned.1.call-update) | async-done | bytes 262160 | tf_op jit(solution)/shard_map/reduce_scatter | solution.py:151
  718.5 10.0 all_to_all.103
  736.2 13.9 collective-permute-done.3
  762.4 39.7 %reduce-scatter.45.cloned.1.call-done = bf16[256,512]{1,0:T(8,128)(2,1)} async-done(((bf16[1024,512]{1,0:T(8,128)(2,1)}), bf16[256,512]{1,0:T(8,128)(2,1)}) %reduce-scatter.45.cloned.1.call-update) | async-done | bytes 262160 | tf_op jit(solution)/shard_map/reduce_scatter | solution.py:151
  827.7 10.0 all_to_all.104
  846.3 13.9 collective-permute-done.4
  871.4 39.8 %reduce-scatter.51.cloned.1.call-done = bf16[256,512]{1,0:T(8,128)(2,1)} async-done(((bf16[1024,512]{1,0:T(8,128)(2,1)}), bf16[256,512]{1,0:T(8,128)(2,1)}) %reduce-scatter.51.cloned.1.call-update) | async-done | bytes 262160 | tf_op jit(solution)/shard_map/reduce_scatter | solution.py:151
  936.9 10.0 all_to_all.105
  956.3 13.9 collective-permute-done.5
  976.3 6.3 fusion.516
  992.0 6.1 fusion.514
  999.9 6.4 multiply_reduce_fusion.18
  1006.4 7.2 multiply_convert_fusion.14
  1067.3 11.8 fusion.394
  1079.1 12.4 fusion.395
  1143.7 10.6 all-to-all-done.6
  1164.3 7.4 all-to-all-done.7
  1173.6 11.3 reduce-scatter.59.cloned.1.call-done
  1192.5 34.9 %psum.37 = f32[1,3,512]{2,0,1:T(1,128)} all-reduce(f32[1,3,512]{2,0,1:T(1,128)S(1)} %broadcast_in_dim.670), channel_id=1, replica_groups=mesh['section'=2,'dp'=4,'mp'=4] {'dp','mp'}, use_global_device_ids=true, to_apply=%region_170.171 | all-reduce | flops 1536 | bytes 12288 | tf_op jit(solution)/shard_map/psum | solution.py:442
  1229.3 281.2 %all-reduce.15.cloned.1.call-done = (bf16[1,512,2,256]{1,3,2,0:T(8,128)(2,1)}, bf16[1,512,2,128]{3,2,1,0:T(2,128)(2,1)}, bf16[1,2,512,2048]{3,2,1,0:T(8,128)(2,1)}, bf16[1,2,2048,512]{3,2,1,0:T(8,128)(2,1)}) async-done(((bf16[1,512,2,256]{1,3,2,0:T(8,128)(2,1)}, bf16[1,512,2,128]{3,2,1,0:T(2,128)(2,1)}, bf16[1,2,512,2048]{3,2,1,0:T(8,128)(2,1)}, bf16[1,2,2048,512]{3,2,1,0:T(8,128)(2,1)}), ...) | async-done | bytes 9175056 | tf_op jit(solution)/shard_map/psum | solution.py:437
  1514.4 6.8 broadcast_in_dim.673
  (924 shorter events, 539.1 us)
Async XLA Ops:
  7.2 25.4 %all-gather.17.cloned.1.call-start = ((), (), s32[]{:S(2)}) async-start(), calls=%async_computation.40 | async-start | bytes 1310720 | tf_op jit(solution)/shard_map/all_gather | solution.py:148
  13.0 57.6 %reduce-scatter.21.cloned.1.call-start = ((), (), s32[]{:S(2)}) async-start(), calls=%async_computation.41 | async-start | bytes 1310720 | tf_op jit(solution)/shard_map/reduce_scatter | solution.py:151
  45.5 46.4 %all-gather.19.cloned.1.call-start = ((), (), s32[]{:S(2)}) async-start(), calls=%async_computation.42 | async-start | bytes 1310720 | tf_op jit(solution)/shard_map/all_gather | solution.py:148
  75.0 56.0 %reduce-scatter.55.cloned.1.call-start = ((), (), s32[]{:S(2)}) async-start(), calls=%async_computation.71 | async-start | bytes 1310720 | tf_op jit(solution)/shard_map/reduce_scatter | solution.py:151
  93.7 65.2 %reduce-scatter.23.cloned.1.call-start = ((), (), s32[]{:S(2)}) async-start(), calls=%async_computation.43 | async-start | bytes 1310720 | tf_op jit(solution)/shard_map/reduce_scatter | solution.py:151
  98.1 80.7 %all-gather.21.cloned.1.call-start = ((), (), s32[]{:S(2)}) async-start(), calls=%async_computation.44 | async-start | bytes 1310720 | tf_op jit(solution)/shard_map/all_gather | solution.py:148
  161.9 68.6 %reduce-scatter.25.cloned.1.call-start = ((), (), s32[]{:S(2)}) async-start(), calls=%async_computation.45 | async-start | bytes 1310720 | tf_op jit(solution)/shard_map/reduce_scatter | solution.py:151
  221.2 29.1 %all-gather.23.cloned.1.call-start = ((), (), s32[]{:S(2)}) async-start(), calls=%async_computation.46 | async-start | bytes 1310720 | tf_op jit(solution)/shard_map/all_gather | solution.py:148
  232.8 35.2 %all-gather.25.cloned.1.call-start = ((), (), s32[]{:S(2)}) async-start(), calls=%async_computation.48 | async-start | bytes 1310720 | tf_op jit(solution)/shard_map/all_gather | solution.py:148
  233.6 62.3 %reduce-scatter.49.cloned.1.call-start = ((), (), s32[]{:S(2)}) async-start(), calls=%async_computation.66 | async-start | bytes 1310720 | tf_op jit(solution)/shard_map/reduce_scatter | solution.py:151
  235.6 14.6 collective-permute-start
  252.9 71.2 %reduce-scatter.27.cloned.1.call-start = ((), (), s32[]{:S(2)}) async-start(), calls=%async_computation.47 | async-start | bytes 1310720 | tf_op jit(solution)/shard_map/reduce_scatter | solution.py:151
  259.7 98.6 %reduce-scatter.29.cloned.1.call-start = ((), (), s32[]{:S(2)}) async-start(), calls=%async_computation.49 | async-start | bytes 1310720 | tf_op jit(solution)/shard_map/reduce_scatter | solution.py:151
  349.7 28.1 %all-gather.27.cloned.1.call-start = ((), (), s32[]{:S(2)}) async-start(), calls=%async_computation.50 | async-start | bytes 1310720 | tf_op jit(solution)/shard_map/all_gather | solution.py:148
  360.6 35.0 %all-gather.29.cloned.1.call-start = ((), (), s32[]{:S(2)}) async-start(), calls=%async_computation.52 | async-start | bytes 1310720 | tf_op jit(solution)/shard_map/all_gather | solution.py:148
  361.2 62.5 %reduce-scatter.43.cloned.1.call-start = ((), (), s32[]{:S(2)}) async-start(), calls=%async_computation.61 | async-start | bytes 1310720 | tf_op jit(solution)/shard_map/reduce_scatter | solution.py:151
  363.3 14.5 collective-permute-start.1
  381.2 70.4 %reduce-scatter.31.cloned.1.call-start = ((), (), s32[]{:S(2)}) async-start(), calls=%async_computation.51 | async-start | bytes 1310720 | tf_op jit(solution)/shard_map/reduce_scatter | solution.py:151
  390.2 94.2 %reduce-scatter.33.cloned.1.call-start = ((), (), s32[]{:S(2)}) async-start(), calls=%async_computation.53 | async-start | bytes 1310720 | tf_op jit(solution)/shard_map/reduce_scatter | solution.py:151
  475.8 27.8 %all-gather.31.cloned.1.call-start = ((), (), s32[]{:S(2)}) async-start(), calls=%async_computation.54 | async-start | bytes 1310720 | tf_op jit(solution)/shard_map/all_gather | solution.py:148
  486.8 58.2 %reduce-scatter.37.cloned.1.call-start = ((), (), s32[]{:S(2)}) async-start(), calls=%async_computation.56 | async-start | bytes 1310720 | tf_op jit(solution)/shard_map/reduce_scatter | solution.py:151
  488.1 14.3 collective-permute-start.2
  505.5 67.5 %reduce-scatter.35.cloned.1.call-start = ((), (), s32[]{:S(2)}) async-start(), calls=%async_computation.55 | async-start | bytes 1310720 | tf_op jit(solution)/shard_map/reduce_scatter | solution.py:151
  611.5 30.3 %all-gather.33.cloned.1.call-start = ((), (), s32[]{:S(2)}) async-start(), calls=%async_computation.57 | async-start | bytes 1310720 | tf_op jit(solution)/shard_map/all_gather | solution.py:148
  624.9 67.8 %reduce-scatter.39.cloned.1.call-start = ((), (), s32[]{:S(2)}) async-start(), calls=%async_computation.58 | async-start | bytes 1310720 | tf_op jit(solution)/shard_map/reduce_scatter | solution.py:151
  650.5 48.9 %all-to-all-start.12 = ((bf16[4,2,48,512]{3,2,1,0:T(8,128)(2,1)}), bf16[4,2,48,512]{3,2,1,0:T(8,128)(2,1)}, u32[]{:S(2)}, u32[]{:S(2)}) async-start(bf16[4,2,48,512]{3,2,1,0:T(8,128)(2,1)} %bitcast.185), calls=%async_computation.24 | async-start | bytes 786432 | tf_op jit(solution)/shard_map/all_to_all | solution.py:156
  702.9 48.6 %all-gather.37.cloned.1.call-start = ((), (), s32[]{:S(2)}) async-start(), calls=%async_computation.62 | async-start | bytes 1310720 | tf_op jit(solution)/shard_map/all_gather | solution.py:148
  734.6 67.5 %reduce-scatter.45.cloned.1.call-start = ((), (), s32[]{:S(2)}) async-start(), calls=%async_computation.63 | async-start | bytes 1310720 | tf_op jit(solution)/shard_map/reduce_scatter | solution.py:151
  734.9 15.2 collective-permute-start.3
  758.9 49.6 %all-to-all-start.15 = ((bf16[4,2,48,512]{3,2,1,0:T(8,128)(2,1)}), bf16[4,2,48,512]{3,2,1,0:T(8,128)(2,1)S(1)}, u32[]{:S(2)}, u32[]{:S(2)}) async-start(bf16[4,2,48,512]{3,2,1,0:T(8,128)(2,1)} %bitcast.200), calls=%async_computation.30 | async-start | bytes 786432 | tf_op jit(solution)/shard_map/all_to_all | solution.py:156
  812.0 48.5 %all-gather.41.cloned.1.call-start = ((), (), s32[]{:S(2)}) async-start(), calls=%async_computation.67 | async-start | bytes 1310720 | tf_op jit(solution)/shard_map/all_gather | solution.py:148
  843.6 67.7 %reduce-scatter.51.cloned.1.call-start = ((), (), s32[]{:S(2)}) async-start(), calls=%async_computation.68 | async-start | bytes 1310720 | tf_op jit(solution)/shard_map/reduce_scatter | solution.py:151
  845.0 15.2 collective-permute-start.4
  868.0 49.8 %all-to-all-start.18 = ((bf16[4,2,48,512]{3,2,1,0:T(8,128)(2,1)}), bf16[4,2,48,512]{3,2,1,0:T(8,128)(2,1)S(1)}, u32[]{:S(2)}, u32[]{:S(2)}) async-start(bf16[4,2,48,512]{3,2,1,0:T(8,128)(2,1)} %bitcast.216), calls=%async_computation.36 | async-start | bytes 786432 | tf_op jit(solution)/shard_map/all_to_all | solution.py:156
  921.2 48.9 %all-gather.45.cloned.1.call-start = ((), (), s32[]{:S(2)}) async-start(), calls=%async_computation.72 | async-start | bytes 1310720 | tf_op jit(solution)/shard_map/all_gather | solution.py:148
  952.8 45.3 %all-gather.35.cloned.1.call-start = ((), (), s32[]{:S(2)}) async-start(), calls=%async_computation.59 | async-start | bytes 1310720 | tf_op jit(solution)/shard_map/all_gather | solution.py:148
  953.6 64.2 %reduce-scatter.57.cloned.1.call-start = ((), (), s32[]{:S(2)}) async-start(), calls=%async_computation.73 | async-start | bytes 1310720 | tf_op jit(solution)/shard_map/reduce_scatter | solution.py:151
  955.0 15.2 collective-permute-start.5
  976.0 69.0 %all-gather.39.cloned.1.call-start = ((), (), s32[]{:S(2)}) async-start(), calls=%async_computation.64 | async-start | bytes 1310720 | tf_op jit(solution)/shard_map/all_gather | solution.py:148
  992.0 99.6 %all-gather.43.cloned.1.call-start = ((), (), s32[]{:S(2)}) async-start(), calls=%async_computation.69 | async-start | bytes 1310720 | tf_op jit(solution)/shard_map/all_gather | solution.py:148
  1006.4 103.7 %all-gather.47.cloned.1.call-start = ((), (), s32[]{:S(2)}) async-start(), calls=%async_computation.74 | async-start | bytes 1310720 | tf_op jit(solution)/shard_map/all_gather | solution.py:148
  1021.6 152.0 %reduce-scatter.41.cloned.1.call-start = ((), (), s32[]{:S(2)}) async-start(), calls=%async_computation.60 | async-start | bytes 1310720 | tf_op jit(solution)/shard_map/reduce_scatter | solution.py:151
  1031.5 142.1 %reduce-scatter.47.cloned.1.call-start = ((), (), s32[]{:S(2)}) async-start(), calls=%async_computation.65 | async-start | bytes 1310720 | tf_op jit(solution)/shard_map/reduce_scatter | solution.py:151
  1061.5 112.1 %reduce-scatter.53.cloned.1.call-start = ((), (), s32[]{:S(2)}) async-start(), calls=%async_computation.70 | async-start | bytes 1310720 | tf_op jit(solution)/shard_map/reduce_scatter | solution.py:151
  1107.9 77.1 %reduce-scatter.59.cloned.1.call-start = ((), (), s32[]{:S(2)}) async-start(), calls=%async_computation.75 | async-start | bytes 1310720 | tf_op jit(solution)/shard_map/reduce_scatter | solution.py:151
  1125.7 384.7 %all-reduce.15.cloned.1.call-start = ((), (), s32[]{:S(2)}) async-start(), calls=%async_computation.76 | async-start | bytes 18350080 | tf_op jit(solution)/shard_map/psum | solution.py:437
  1140.1 14.2 all-to-all-start.6
  1160.5 11.1 all-to-all-start.7
  (226 other events, 4652.2 us)
Sparse Core Ops, SparseCore 0:
  13.1 19.3 all-gather.16
  45.6 24.8 reduce-scatter.20
  75.1 16.7 all-gather.18
  95.0 35.9 reduce-scatter.54
  134.0 24.8 reduce-scatter.22
  162.0 16.7 all-gather.20
  195.6 24.8 reduce-scatter.24
  232.9 16.7 all-gather.22
  251.3 16.7 all-gather.24
  271.0 24.8 reduce-scatter.48
  299.2 24.8 reduce-scatter.26
  326.5 24.8 reduce-scatter.28
  360.8 16.5 all-gather.26
  378.9 16.7 all-gather.28
  398.7 24.8 reduce-scatter.42
  426.6 24.8 reduce-scatter.30
  454.1 24.8 reduce-scatter.32
  486.9 16.6 all-gather.30
  506.7 38.2 reduce-scatter.36
  548.1 24.8 reduce-scatter.34
  625.1 16.7 all-gather.32
  646.8 45.9 reduce-scatter.38
  734.7 16.7 all-gather.36
  755.4 46.5 reduce-scatter.44
  843.7 16.7 all-gather.40
  864.4 46.8 reduce-scatter.50
  953.0 16.7 all-gather.44
  971.4 16.7 all-gather.34
  991.4 24.8 reduce-scatter.56
  1017.7 16.7 all-gather.38
  1036.1 16.7 all-gather.42
  1054.4 16.7 all-gather.46
  1074.1 24.9 reduce-scatter.40
  1101.8 24.8 reduce-scatter.46
  1129.8 27.7 reduce-scatter.52
  1160.7 24.2 reduce-scatter.58
  1188.3 322.0 all-reduce.14
where the time goes:
time: 1540 us; the launch traced here: 1530 us
  waiting for transfers between devices  857 us (56%)
  matrix products  270 us (18%)
  local copies, waits for them, and re-layouts  113 us (7%)
  other arithmetic  111 us (7%)
  blocking collectives  95.7 us (6%)
  starting transfers between devices  68.1 us (4%)
  between operations  18.4 us (1%)
    reduce_scatter x20, waiting for transfers between devices, spread(): lax.psum_scatter(partial_sum.astype(jnp.bfloat16), 'mp', scatter_dimensio...  359 us
    psum x1, waiting for transfers between devices, on_device(): lax.psum(self_total.astype(jnp.bfloat16), 'dp').astype(jnp.float32)  281 us
    all_gather x16, waiting for transfers between devices, collect(): return lax.all_gather(piece, 'mp', axis=0, tiled=True)  80.7 us
    ppermute x6, waiting for transfers between devices, shifted(): return lax.ppermute(shard, axis, pairs)  74.3 us
    all_to_all x6, blocking collectives, route(): return lax.all_to_all(buffer, 'mp', split_axis=0, concat_axis=0, tiled=True)  60.8 us
    all_to_all x14, waiting for transfers between devices, route(): return lax.all_to_all(buffer, 'mp', split_axis=0, concat_axis=0, tiled=True)  59.1 us
    all_to_all x14, starting transfers between devices, route(): return lax.all_to_all(buffer, 'mp', split_axis=0, concat_axis=0, tiled=True)  49.5 us
    psum x1, blocking collectives, on_device(): gain_total = lax.psum(gain_total, ('dp', 'mp'))  34.9 us
  transfers between devices with their start and end apart: 57, of which 40 were waited for; matrix products, arithmetic and copies ran while one was open for 22% of the time, Pallas kernels for 0%

commit v1 on v0

v1 whole, which is shorter than its diff:
```python
import functools

import jax
import jax.numpy as jnp
from jax import lax
from jax.experimental import pallas as pl
from jax.experimental.pallas import tpu as pltpu
from jax.sharding import PartitionSpec as P

SEQ = 1024
EPS = 1e-05
NEG = -1000000000.0
BF = jnp.bfloat16
F32 = jnp.float32
QB = 256


def dot(a, b, ca=1, cb=0):
    return lax.dot_general(a, b, (((ca,), (cb,)), ((), ())), preferred_element_type=F32)


def norm_parts(rows):
    centred = rows - jnp.mean(rows, axis=-1, keepdims=True)
    inverse = lax.rsqrt(jnp.mean(centred * centred, axis=-1, keepdims=True) + EPS)
    return centred * inverse, inverse


def norm_back(upstream, unit, inverse, gain):
    scaled = upstream * gain
    inner = (
        scaled
        - jnp.mean(scaled, axis=-1, keepdims=True)
        - unit * jnp.mean(scaled * unit, axis=-1, keepdims=True)
    )
    return inverse * inner, jnp.sum(upstream * unit, axis=0, keepdims=True)


def gelu_parts(z):
    square = z * z
    t = jnp.tanh(z * (0.7978845608028654 + (0.7978845608028654 * 0.044715) * square))
    half = 0.5 + 0.5 * t
    slope = half + (0.5 * z) * (1.0 - t * t) * (
        0.7978845608028654 + (3.0 * 0.7978845608028654 * 0.044715) * square
    )
    return z * half, slope


def gelu_value(z):
    t = jnp.tanh(z * (0.7978845608028654 + (0.7978845608028654 * 0.044715) * (z * z)))
    return z * (0.5 + 0.5 * t)


def causal_keep(rows, cols, first):
    r = lax.broadcasted_iota(jnp.int32, (rows, cols), 0) + first
    return lax.broadcasted_iota(jnp.int32, (rows, cols), 1) <= r


def attend_tile(q, k, v, first):
    s = dot(q, k, 1, 1) * (q.shape[1] ** -0.5)
    if first is not None:
        s = jnp.where(causal_keep(s.shape[0], s.shape[1], first), s, NEG)
    peak = jnp.max(s, axis=-1, keepdims=True)
    p = jnp.exp(s - peak)
    total = jnp.sum(p, axis=-1, keepdims=True)
    o = dot(p.astype(BF), v) / total
    return o.astype(BF), peak + jnp.log(total)


def attend_tile_back(q, k, v, do, o, lse, first):
    scale = q.shape[1] ** -0.5
    s = dot(q, k, 1, 1) * scale
    if first is not None:
        s = jnp.where(causal_keep(s.shape[0], s.shape[1], first), s, NEG)
    p = jnp.exp(s - lse)
    inner = jnp.sum(do.astype(F32) * o.astype(F32), axis=-1, keepdims=True)
    dp = dot(do, v, 1, 1)
    ds = (p * (dp - inner)).astype(BF)
    dq = dot(ds, k) * scale
    dk = dot(ds, q, 0, 0) * scale
    dv = dot(p.astype(BF), do, 0, 0)
    return dq, dk, dv


def params(mb=48):
    return pltpu.CompilerParams(vmem_limit_bytes=mb << 20)


SM = pl.BlockSpec(memory_space=pltpu.SMEM)
VM = pl.BlockSpec(memory_space=pltpu.VMEM)


def call(body, scal, ins, outs, scratch=(), flops=0, mb=48):
    shapes = [jax.ShapeDtypeStruct(s, d) for s, d in outs]
    moved = sum(a.size * a.dtype.itemsize for a in list(ins) + shapes)
    return pl.pallas_call(
        body,
        out_shape=shapes,
        in_specs=[SM] + [VM] * len(ins),
        out_specs=[VM] * len(outs),
        scratch_shapes=list(scratch),
        compiler_params=params(mb),
        cost_estimate=pl.CostEstimate(flops=flops, bytes_accessed=moved, transcendentals=0),
    )(scal, *ins)


def place_body(n, el, capp, scal, labels, out):
    me = scal[0]
    tokens = labels.shape[1]
    r = lax.broadcasted_iota(jnp.int32, (tokens, tokens), 0)
    c = lax.broadcasted_iota(jnp.int32, (tokens, tokens), 1)
    lower = (c < r).astype(BF)
    experts = n * el
    for m in range(labels.shape[0]):
        lab = labels[m]
        hot = lab == lax.broadcasted_iota(jnp.int32, (tokens, experts), 1)
        hot = jnp.where(hot, 1.0, 0.0)
        before = dot(lower, hot.astype(BF))
        slot = jnp.sum(before * hot, axis=1, keepdims=True).astype(jnp.int32)
        where = ((lab // el) ^ me) * (el * capp) + (lab % el) * capp + slot
        wide = jnp.where(
            where == lax.broadcasted_iota(jnp.int32, (tokens, n * el * capp), 1), 1.0, 0.0
        )
        out[m] = wide.T.astype(BF)


def send_slots(d_ref, rows, outs):
    size = outs[0].shape[0]
    for j, out in enumerate(outs):
        out[...] = dot(d_ref[j * size : (j + 1) * size, :], rows).astype(BF)


def self_fwd_body(n, hl, hs, scal, *refs):
    xs, (g, w), refs = refs[:n], refs[n : n + 2], refs[n + 2 :]
    a, qkv, o, lse = refs[:4]
    parts = refs[4:]
    me, dec = scal[0], scal[1]
    tokens = xs[0].shape[0]
    group = n * tokens
    hw = hl * hs
    for j in range(n):
        unit, _ = norm_parts(xs[j][...].astype(F32))
        a[pl.ds((me ^ j) * tokens, tokens), :] = (unit * g[...]).astype(BF)
    qkv[...] = dot(a[...], w[:, : 3 * hw]).astype(BF)

    def run(causal):
        lane = lax.broadcasted_iota(jnp.int32, (QB, 128), 1)
        for base in range(0, group, SEQ):
            for first in range(0, SEQ, QB):
                rows = slice(base + first, base + first + QB)
                keys = slice(base, base + (first + QB if causal else SEQ))
                stats = jnp.zeros((QB, 128), F32)
                for h in range(hl):
                    q = qkv[rows, h * hs : (h + 1) * hs]
                    k = qkv[keys, hw + h * hs : hw + (h + 1) * hs]
                    v = qkv[keys, 2 * hw + h * hs : 2 * hw + (h + 1) * hs]
                    out, logs = attend_tile(q, k, v, first if causal else None)
                    o[rows, h * hs : (h + 1) * hs] = out
                    stats = jnp.where(lane == h, logs, stats)
                lse[rows, :] = stats

    pl.when(dec == 1)(lambda: run(True))
    pl.when(dec == 0)(lambda: run(False))
    for j in range(n):
        rows = o[pl.ds((me ^ j) * tokens, tokens), :]
        parts[j][...] = dot(rows, w[:, 3 * hw :], 1, 1).astype(BF)


def self_bwd_body(n, hl, hs, scal, *refs):
    gs, refs = refs[:n], refs[n:]
    a, qkv, o, lse, g, w = refs[:6]
    parts, (dw, dgain), (dso, do, dqkv, acc) = refs[6 : 6 + n], refs[6 + n : 8 + n], refs[8 + n :]
    me, dec = scal[0], scal[1]
    tokens = gs[0].shape[0]
    group = n * tokens
    hw = hl * hs
    for j in range(n):
        dso[pl.ds((me ^ j) * tokens, tokens), :] = gs[j][...]
    do[...] = dot(dso[...], w[:, 3 * hw :]).astype(BF)

    def run(causal):
        for base in range(0, group, SEQ):
            for h in range(hl):
                acc[...] = jnp.zeros_like(acc)
                for first in range(0, SEQ, QB):
                    rows = slice(base + first, base + first + QB)
                    width = first + QB if causal else SEQ
                    keys = slice(base, base + width)
                    cols = slice(h * hs, (h + 1) * hs)
                    k = qkv[keys, hw + h * hs : hw + (h + 1) * hs]
                    v = qkv[keys, 2 * hw + h * hs : 2 * hw + (h + 1) * hs]
                    dq, dk, dv = attend_tile_back(
                        qkv[rows, cols],
                        k,
                        v,
                        do[rows, cols],
                        o[rows, cols],
                        lse[rows, h : h + 1],
                        first if causal else None,
                    )
                    dqkv[rows, cols] = dq.astype(BF)
                    acc[0, :width, :] += dk
                    acc[1, :width, :] += dv
                keys = slice(base, base + SEQ)
                dqkv[keys, hw + h * hs : hw + (h + 1) * hs] = acc[0].astype(BF)
                dqkv[keys, 2 * hw + h * hs : 2 * hw + (h + 1) * hs] = acc[1].astype(BF)

    pl.when(dec == 1)(lambda: run(True))
    pl.when(dec == 0)(lambda: run(False))
    total = jnp.zeros((1, a.shape[1]), F32)
    for j in range(n):
        rows = pl.ds((me ^ j) * tokens, tokens)
        da = dot(dqkv[rows, :], w[:, : 3 * hw], 1, 1)
        parts[j][...] = da.astype(BF)
        total += jnp.sum(da * a[rows, :].astype(F32), axis=0, keepdims=True)
    dgain[...] = total / g[...]
    dw[:, : 3 * hw] = dot(a[...], dqkv[...], 0, 0)
    dw[:, 3 * hw :] = dot(dso[...], o[...], 0, 0)


def after_self_body(n, pieces, scal, *refs):
    x, refs = refs[0], refs[1:]
    ps, (g2, d, cot), (h1,), outs = (
        refs[:pieces],
        refs[pieces : pieces + 3],
        refs[pieces + 3 : pieces + 4],
        refs[pieces + 4 :],
    )
    rows = x[...].astype(F32)
    for p in ps:
        rows = rows + p[...].astype(F32)
    h1[...] = rows
    unit, _ = norm_parts(rows)
    u = (unit * g2[...]).astype(BF)
    chosen = jnp.where(scal[1] == 0, u.astype(F32), cot[...].astype(F32)).astype(BF)
    send_slots(d, chosen, outs)


def memory_body(n, scal, *refs):
    rs, (h1, d, g1), (y, m) = refs[:n], refs[n : n + 3], refs[n + 3 :]

    @pl.when(scal[1] == 0)
    def _():
        stacked = jnp.concatenate([r[...] for r in rs], axis=0)
        rows = h1[...] + dot(d[...], stacked, 0, 0)
        y[...] = rows
        unit, _ = norm_parts(rows)
        m[...] = (unit * g1[...]).astype(BF)


def final_body(n, scal, *refs):
    rs, (h2, d, ye), (out,) = refs[:n], refs[n : n + 3], refs[n + 3 :]

    @pl.when(scal[1] == 0)
    def _():
        out[...] = ye[...].astype(BF)

    @pl.when(scal[1] == 1)
    def _():
        stacked = jnp.concatenate([r[...] for r in rs], axis=0)
        out[...] = (h2[...] + dot(d[...], stacked, 0, 0)).astype(BF)


def cross_fwd_body(n, per, hl, hs, scal, *refs):
    ms, wx, wkv = refs[:per], refs[per : per + n], refs[per + n : per + 2 * n]
    h1, g1, g2, d = refs[per + 2 * n : per + 2 * n + 4]
    refs = refs[per + 2 * n + 4 :]
    h2, c, mem, qc, kv, oc, lse = refs[:7]
    outs = refs[7:]
    hw = hl * hs
    tokens = h1.shape[0]

    @pl.when(scal[1] == 1)
    def _():
        for j in range(per):
            mem[j * tokens : (j + 1) * tokens, :] = ms[j][...]
        unit, _ = norm_parts(h1[...])
        c[...] = (unit * g1[...]).astype(BF)
        stats = jnp.zeros((tokens, 128), F32)
        lane = lax.broadcasted_iota(jnp.int32, (tokens, 128), 1)
        total = h1[...]
        for j in range(n):
            qc[:, j * hw : (j + 1) * hw] = dot(c[...], wx[j][:, :hw]).astype(BF)
            kv[:, 2 * j * hw : 2 * (j + 1) * hw] = dot(mem[...], wkv[j][...]).astype(BF)
            for h in range(hl):
                at = j * hw + h * hs
                k = kv[:, 2 * j * hw + h * hs : 2 * j * hw + (h + 1) * hs]
                v = kv[:, (2 * j + 1) * hw + h * hs : (2 * j + 1) * hw + (h + 1) * hs]
                out, logs = attend_tile(qc[:, at : at + hs], k, v, None)
                oc[:, at : at + hs] = out
                stats = jnp.where(lane == j * hl + h, logs, stats)
            total = total + dot(oc[:, j * hw : (j + 1) * hw], wx[j][:, hw:], 1, 1)
        lse[...] = stats
        h2[...] = total
        unit, _ = norm_parts(total)
        send_slots(d, (unit * g2[...]).astype(BF), outs)


def cross_bwd_body(n, per, hl, hs, scal, *refs):
    dus, wx, wkv = refs[:n], refs[n : 2 * n], refs[2 * n : 3 * n]
    h2, g2, d, cot, qc, kv, oc, lse = refs[3 * n : 3 * n + 8]
    refs = refs[3 * n + 8 :]
    dh2, dco, dqc, dkv, dgain = refs[:5]
    dms, (doc,) = refs[5 : 5 + per], refs[5 + per :]
    hw = hl * hs
    tokens = h2.shape[0]

    @pl.when(scal[1] == 0)
    def _():
        dgain[...] = jnp.zeros_like(dgain)

    @pl.when(scal[1] == 1)
    def _():
        stacked = jnp.concatenate([r[...] for r in dus], axis=0)
        unit, inverse = norm_parts(h2[...])
        back, gained = norm_back(dot(d[...], stacked, 0, 0), unit, inverse, g2[...])
        dgain[...] = gained
        total = cot[...].astype(F32) + back
        dh2[...] = total
        dco[...] = total.astype(BF)
        for j in range(n):
            doc[:, j * hw : (j + 1) * hw] = dot(dco[...], wx[j][:, hw:]).astype(BF)
            for h in range(hl):
                at = j * hw + h * hs
                k = slice(2 * j * hw + h * hs, 2 * j * hw + (h + 1) * hs)
                v = slice((2 * j + 1) * hw + h * hs, (2 * j + 1) * hw + (h + 1) * hs)
                dq, dk, dv = attend_tile_back(
                    qc[:, at : at + hs],
                    kv[:, k],
                    kv[:, v],
                    doc[:, at : at + hs],
                    oc[:, at : at + hs],
                    lse[:, j * hl + h : j * hl + h + 1],
                    None,
                )
                dqc[:, at : at + hs] = dq.astype(BF)
                dkv[:, k] = dk.astype(BF)
                dkv[:, v] = dv.astype(BF)
        for i in range(per):
            rows = slice(i * tokens, (i + 1) * tokens)
            total = 0.0
            for j in range(n):
                total += dot(dkv[rows, 2 * j * hw : 2 * (j + 1) * hw], wkv[j][...], 1, 1)
            dms[i][...] = total.astype(BF)


def cross_late_body(n, hl, hs, scal, *refs):
    wx = refs[:n]
    dh2, dco, dqc, dkv, oc, c, mem, h1, g1 = refs[n : n + 9]
    dh1, dwx, dwkv, dgain = refs[n + 9 :]
    hw = hl * hs

    @pl.when(scal[1] == 1)
    def _():
        dc = jnp.zeros(h1.shape, F32)
        for j in range(n):
            dc += dot(dqc[:, j * hw : (j + 1) * hw], wx[j][:, :hw], 1, 1)
        unit, inverse = norm_parts(h1[...])
        back, gained = norm_back(dc, unit, inverse, g1[...])
        dh1[...] = dh2[...] + back
        dgain[...] = gained
        dq = dot(c[...], dqc[...], 0, 0)
        de = dot(dco[...], oc[...], 0, 0)
        for j in range(n):
            dwx[j, :, :hw] = dq[:, j * hw : (j + 1) * hw]
            dwx[j, :, hw:] = de[:, j * hw : (j + 1) * hw]
        dk = dot(mem[...], dkv[...], 0, 0)
        for j in range(n):
            dwkv[j] = dk[:, 2 * j * hw : 2 * (j + 1) * hw]


def memory_back_body(n, pieces, scal, *refs):
    ps, (y, g1, cot, d), (dy, dgain), outs = (
        refs[:pieces],
        refs[pieces : pieces + 4],
        refs[pieces + 4 : pieces + 6],
        refs[pieces + 6 :],
    )

    @pl.when(scal[1] == 0)
    def _():
        dm = ps[0][...].astype(F32)
        for p in ps[1:]:
            dm = dm + p[...].astype(F32)
        unit, inverse = norm_parts(y[...])
        back, gained = norm_back(dm, unit, inverse, g1[...])
        dgain[...] = gained
        rows = cot[...].astype(F32) + back
        dy[...] = rows
        send_slots(d, rows.astype(BF), outs)


def before_self_body(n, scal, *refs):
    dus, (d, dy, h1, g2, given), (dh1, dso, dgain) = refs[:n], refs[n : n + 5], refs[n + 5 :]

    @pl.when(scal[1] == 0)
    def _():
        stacked = jnp.concatenate([r[...] for r in dus], axis=0)
        unit, inverse = norm_parts(h1[...])
        back, gained = norm_back(dot(d[...], stacked, 0, 0), unit, inverse, g2[...])
        rows = dy[...] + back
        dh1[...] = rows
        dso[...] = rows.astype(BF)
        dgain[...] = gained

    @pl.when(scal[1] == 1)
    def _():
        dh1[...] = given[...]
        dso[...] = given[...].astype(BF)
        dgain[...] = jnp.zeros_like(dgain)


def finish_body(pieces, scal, *refs):
    ps, (dh1, x, g0), (out,) = refs[:pieces], refs[pieces : pieces + 3], refs[pieces + 3 :]
    da = ps[0][...].astype(F32)
    for p in ps[1:]:
        da = da + p[...].astype(F32)
    unit, inverse = norm_parts(x[...].astype(F32))
    back, _ = norm_back(da, unit, inverse, g0[...])
    out[...] = dh1[...] + back


def expert_body(n, el, capp, steps, active, mode, scal, *refs):
    us, refs = refs[:n], refs[n:]
    drs = ()
    if mode != "fwd":
        drs, refs = refs[:n], refs[n:]
    (wi, wo), refs = refs[:2], refs[2:]
    rs, dus = (), ()
    if mode != "back":
        rs, refs = refs[:n], refs[n:]
    if mode != "fwd":
        dus, refs = refs[:n], refs[n:]
    scratch = list(refs)
    e, f = pl.program_id(0), pl.program_id(1)
    u = scratch.pop(0)
    dr = scratch.pop(0) if drs else None
    racc = scratch.pop(0) if rs else None
    dacc = scratch.pop(0) if dus else None

    @pl.when(scal[1] == active)
    def _():
        at = pl.ds(pl.multiple_of(e * capp, 16), capp)

        @pl.when(f == 0)
        def _():
            for j in range(n):
                u[j * capp : (j + 1) * capp, :] = us[j][at, :]
                if drs:
                    dr[j * capp : (j + 1) * capp, :] = drs[j][at, :]
            if rs:
                racc[...] = jnp.zeros_like(racc)
            if dus:
                dacc[...] = jnp.zeros_like(dacc)

        z = dot(u[...], wi[0])
        if not drs:
            g = gelu_value(z)
        else:
            g, slope = gelu_parts(z)
        if rs:
            racc[...] += dot(g.astype(BF), wo[0])
        if dus:
            dg = dot(dr[...], wo[0], 1, 1)
            dz = (dg * slope).astype(BF)
            dacc[...] += dot(dz, wi[0], 1, 1)

        @pl.when(f == steps - 1)
        def _():
            for j in range(n):
                if rs:
                    rs[j][at, :] = racc[j * capp : (j + 1) * capp, :].astype(BF)
                if dus:
                    dus[j][at, :] = dacc[j * capp : (j + 1) * capp, :].astype(BF)


def experts(scal, us, drs, w_in, w_out, capp, active, mode):
    n, el = len(us), w_in.shape[0]
    width, ff = w_in.shape[1:]
    block = 512
    steps = ff // block
    rows = n * capp
    whole = pl.BlockSpec((el * capp, width), lambda e, f, s: (0, 0))

    def on(s):
        return jnp.where(s[1] == active, 1, 0)

    outs = n * (2 if mode == "both" else 1)
    scratch = [pltpu.VMEM((rows, width), BF)] * (1 if mode == "fwd" else 2)
    scratch += [pltpu.VMEM((rows, width), F32)] * (2 if mode == "both" else 1)
    products = {"fwd": 2, "both": 4, "back": 3}[mode]
    result = pl.pallas_call(
        functools.partial(expert_body, n, el, capp, steps, active, mode),
        grid_spec=pltpu.PrefetchScalarGridSpec(
            num_scalar_prefetch=1,
            grid=(el, steps),
            in_specs=[whole] * (len(us) + len(drs))
            + [
                pl.BlockSpec((1, width, block), lambda e, f, s: (e * on(s), 0, f * on(s))),
                pl.BlockSpec((1, block, width), lambda e, f, s: (e * on(s), f * on(s), 0)),
            ],
            out_specs=[whole] * outs,
            scratch_shapes=scratch,
        ),
        out_shape=[jax.ShapeDtypeStruct((el * capp, width), BF)] * outs,
        compiler_params=params(),
        cost_estimate=pl.CostEstimate(
            flops=products * 2 * el * rows * width * ff,
            bytes_accessed=2 * 2 * el * width * ff,
            transcendentals=0,
        ),
    )(scal, *us, *drs, w_in, w_out)
    return [result[i : i + n] for i in range(0, outs, n)]


def expert_grad_body(micro, chunk, *refs):
    us, drs, (wi, wo), (dwi, dwo) = (
        refs[:micro],
        refs[micro : 2 * micro],
        refs[2 * micro : 2 * micro + 2],
        refs[2 * micro + 2 :],
    )
    lead, _, capp, width = us[0].shape
    first = True
    for m in range(micro):
        for at in range(0, lead, chunk):
            u = us[m][at : at + chunk, 0].reshape(chunk * capp, width)
            dr = drs[m][at : at + chunk, 0].reshape(chunk * capp, width)
            z = dot(u, wi[0])
            g, slope = gelu_parts(z)
            dz = (dot(dr, wo[0], 1, 1) * slope).astype(BF)
            di = dot(u, dz, 0, 0)
            do = dot(g.astype(BF), dr, 0, 0)
            if first:
                dwi[0] = di
                dwo[0] = do
            else:
                dwi[0] += di
                dwo[0] += do
            first = False


def expert_grads(us, drs, w_in, w_out):
    micro = len(us)
    lead, el, capp, width = us[0].shape
    ff = w_in.shape[2]
    block = 256
    chunk = min(lead, max(1, 768 // capp))
    while lead % chunk:
        chunk -= 1
    rows = pl.BlockSpec((lead, 1, capp, width), lambda e, f: (0, e, 0, 0))
    into = pl.BlockSpec((1, width, block), lambda e, f: (e, 0, f))
    back = pl.BlockSpec((1, block, width), lambda e, f: (e, f, 0))
    return pl.pallas_call(
        functools.partial(expert_grad_body, micro, chunk),
        grid=(el, ff // block),
        in_specs=[rows] * (2 * micro) + [into, back],
        out_specs=[into, back],
        out_shape=[jax.ShapeDtypeStruct(w_in.shape, F32), jax.ShapeDtypeStruct(w_out.shape, F32)],
        compiler_params=params(),
        cost_estimate=pl.CostEstimate(
            flops=8 * micro * lead * el * capp * width * ff,
            bytes_accessed=6 * 2 * el * width * ff,
            transcendentals=0,
        ),
    )(*us, *drs, w_in, w_out)


def on_device(inputs, cotangent, expert_ids, self_proj, cross_proj, gains, w_in, w_out):
    micro, tokens, width = inputs.shape[1:]
    n = lax.axis_size("mp")
    dps = lax.axis_size("dp")
    hl = self_proj.shape[2]
    hs = self_proj.shape[3] // 4
    hw = hl * hs
    el = w_in.shape[1]
    capacity = max(2, 3 * tokens // (2 * n * el))
    capp = -(-capacity // 16) * 16
    slots = el * capp
    per = SEQ // tokens
    group = n * tokens
    me = lax.axis_index("mp")
    decoder = lax.axis_index("section") == 1
    scal = jnp.stack([me, lax.axis_index("section")]).astype(jnp.int32)
    first_weight, second_weight = w_in[0], w_out[0]
    gain = [gains[0, i : i + 1] for i in range(3)]
    ENC, DEC, ALL = (0,), (1,), (0, 1)

    def swap(x, k, sections=ALL):
        pairs = [(s * n + i, s * n + (i ^ k)) for s in sections for i in range(n)]
        return lax.ppermute(x, ("section", "mp"), pairs)

    def gather(x, count, sections=ALL):
        blocks = {0: x}
        bit = count // 2
        while bit:
            blocks.update({j ^ bit: swap(b, bit, sections) for j, b in list(blocks.items())})
            bit //= 2
        return [blocks[j] for j in range(count)]

    def scatter(blocks, sections=ALL):
        live = {j: [b] for j, b in enumerate(blocks)}
        bit = 1
        while bit < len(blocks):
            for j in [j for j in live if j & bit]:
                pieces = live.pop(j)
                out = pieces[0]
                if len(pieces) > 1:
                    out = sum(p.astype(F32) for p in pieces).astype(BF)
                live[j ^ bit].append(swap(out, bit, sections))
            bit *= 2
        return live[0]

    def exchange(blocks, sections=ALL):
        return [blocks[0]] + [swap(blocks[j], j, sections) for j in range(1, n)]

    def to_decoder(x):
        return lax.ppermute(x, "section", [(0, 1)])

    def to_encoder(x):
        return lax.ppermute(x, "section", [(1, 0)])

    xs = [inputs[0, m] for m in range(micro)]
    cots = [cotangent[0, m] for m in range(micro)]
    ws = self_proj[0].reshape(width, hl, 4, hs).transpose(0, 2, 1, 3).reshape(width, 4 * hw)
    wc = cross_proj[0].reshape(width, hl, 2, hs).transpose(0, 2, 1, 3).reshape(width, 2 * hw)
    routes = call(
        functools.partial(place_body, n, el, capp),
        scal,
        [expert_ids[0]],
        [((micro, n * slots, tokens), BF)],
    )[0]
    routes = [routes[m] for m in range(micro)]
    M = range(micro)

    row, wide = ((tokens, width), BF), ((tokens, width), F32)
    x_all = [gather(xs[m], n) for m in M]
    saved, self_parts = [], []
    for m in M:
        res = call(
            functools.partial(self_fwd_body, n, hl, hs),
            scal,
            [*x_all[m], gain[0], ws],
            [((group, width), BF), ((group, 3 * hw), BF), ((group, hw), BF), ((group, 128), F32)]
            + [row] * n,
            flops=2 * group * width * 4 * hw + 4 * 4 * group * SEQ * hw,
        )
        saved.append(res[:4])
        self_parts.append(scatter(res[4:]))
    h1, first_slots = [], []
    for m in M:
        res = call(
            functools.partial(after_self_body, n, len(self_parts[m])),
            scal,
            [xs[m], *self_parts[m], gain[2], routes[m], cots[m]],
            [wide] + [((slots, width), BF)] * n,
            flops=2 * n * slots * tokens * width,
        )
        h1.append(res[0])
        first_slots.append(exchange(res[1:]))

    wx_all = gather(wc, n, DEC)
    wkv_all = gather(to_decoder(wc), n, DEC)
    ye, mem_all = [], []
    for m in M:
        (r,) = experts(scal, first_slots[m], (), first_weight, second_weight, capp, 0, "fwd")
        r = exchange(r, ENC)
        y, mem = call(
            functools.partial(memory_body, n),
            scal,
            [*r, h1[m], routes[m], gain[1]],
            [wide, row],
            flops=2 * n * slots * tokens * width,
        )
        ye.append(y)
        mem_all.append(gather(to_decoder(mem), per, DEC))

    crossed, second_slots = [], []
    for m in M:
        res = call(
            functools.partial(cross_fwd_body, n, per, hl, hs),
            scal,
            [*mem_all[m], *wx_all, *wkv_all, h1[m], gain[1], gain[2], routes[m]],
            [
                wide,
                row,
                ((SEQ, width), BF),
                ((tokens, n * hw), BF),
                ((SEQ, 2 * n * hw), BF),
                ((tokens, n * hw), BF),
                ((tokens, 128), F32),
            ]
            + [((slots, width), BF)] * n,
            flops=4 * SEQ * width * n * hw + 4 * 4 * tokens * SEQ * n * hw,
        )
        crossed.append(res[:7])
        second_slots.append(exchange(res[7:], DEC))

    outs, dus = [], []
    for m in M:
        r, du = experts(
            scal, second_slots[m], first_slots[m], first_weight, second_weight, capp, 1, "both"
        )
        dus.append(exchange(du, DEC))
        r = exchange(r, DEC)
        outs.append(
            call(
                functools.partial(final_body, n),
                scal,
                [*r, crossed[m][0], routes[m], ye[m]],
                [row],
            )[0]
        )

    dms, late, gain_parts = [], [], [[], [], []]
    for m in M:
        h2, c, mem, qc, kv, oc, lse = crossed[m]
        res = call(
            functools.partial(cross_bwd_body, n, per, hl, hs),
            scal,
            [*dus[m], *wx_all, *wkv_all, h2, gain[2], routes[m], cots[m], qc, kv, oc, lse],
            [
                wide,
                row,
                ((tokens, n * hw), BF),
                ((SEQ, 2 * n * hw), BF),
                ((1, width), F32),
            ]
            + [row] * per,
            scratch=[pltpu.VMEM((tokens, n * hw), BF)],
            flops=4 * SEQ * width * n * hw + 4 * 10 * tokens * SEQ * n * hw,
        )
        dh2, dco, dqc, dkv, gained = res[:5]
        gain_parts[2].append(gained)
        pieces = scatter(res[5:], DEC)
        dms.append(to_encoder(sum(p.astype(F32) for p in pieces).astype(BF)))
        late.append(
            call(
                functools.partial(cross_late_body, n, hl, hs),
                scal,
                [*wx_all, dh2, dco, dqc, dkv, oc, c, mem, h1[m], gain[1]],
                [
                    wide,
                    ((n, width, 2 * hw), F32),
                    ((n, width, 2 * hw), F32),
                    ((1, width), F32),
                ],
                flops=8 * SEQ * width * n * hw,
            )
        )

    dys, third_slots, memory_gain = [], [], []
    for m in M:
        res = call(
            functools.partial(memory_back_body, n, 1),
            scal,
            [dms[m], ye[m], gain[1], cots[m], routes[m]],
            [wide, ((1, width), F32)] + [((slots, width), BF)] * n,
        )
        dys.append(res[0])
        memory_gain.append(res[1])
        third_slots.append(exchange(res[2:], ENC))
    dh1, dso = [], []
    for m in M:
        (du,) = experts(
            scal, first_slots[m], third_slots[m], first_weight, second_weight, capp, 0, "back"
        )
        du = exchange(du, ENC)
        res = call(
            functools.partial(before_self_body, n),
            scal,
            [*du, routes[m], dys[m], h1[m], gain[2], late[m][0]],
            [wide, row, ((1, width), F32)],
        )
        dh1.append(res[0])
        dso.append(gather(res[1], n))
        gain_parts[2].append(res[2])

    def rows_of(blocks):
        whole = jnp.stack(blocks).reshape(n, el, capp, width)
        return lax.all_gather(whole, "dp", axis=0, tiled=True)

    u_rows = [
        rows_of([jnp.where(decoder, b, a) for a, b in zip(first_slots[m], second_slots[m])])
        for m in M
    ]
    dr_rows = [
        rows_of([jnp.where(decoder, b, a) for a, b in zip(third_slots[m], first_slots[m])])
        for m in M
    ]

    input_grads, self_grads = [], []
    for m in M:
        a, qkv, o, lse = saved[m]
        res = call(
            functools.partial(self_bwd_body, n, hl, hs),
            scal,
            [*dso[m], a, qkv, o, lse, gain[0], ws],
            [row] * n + [((width, 4 * hw), F32), ((1, width), F32)],
            scratch=[
                pltpu.VMEM((group, width), BF),
                pltpu.VMEM((group, hw), BF),
                pltpu.VMEM((group, 3 * hw), BF),
                pltpu.VMEM((2, SEQ, hs), F32),
            ],
            flops=2 * group * width * 8 * hw + 4 * 10 * group * SEQ * hw,
        )
        pieces = scatter(res[:n])
        self_grads.append(res[n])
        gain_parts[0].append(res[n + 1])
        input_grads.append(
            call(
                functools.partial(finish_body, len(pieces)),
                scal,
                [*pieces, dh1[m], xs[m], gain[0]],
                [wide],
            )[0]
        )

    def small_sum(x):
        for axis in ("mp", "dp"):
            count = lax.axis_size(axis)
            bit = 1
            while bit < count:
                x = x + lax.ppermute(x, axis, [(i, i ^ bit) for i in range(count)])
                bit *= 2
        return x

    gain_parts[1] = [jnp.where(decoder, late[m][3], memory_gain[m]) for m in M]
    gain_total = small_sum(jnp.concatenate([sum(p) for p in gain_parts], axis=0))

    self_total = sum(self_grads).astype(BF)
    self_total = lax.psum(self_total, "dp").astype(F32)
    dwx = sum(late[m][1] for m in M).astype(BF)
    dwkv = sum(late[m][2] for m in M).astype(BF)
    dwx = sum(p.astype(F32) for p in scatter([dwx[j] for j in range(n)], DEC)).astype(BF)
    dwkv = sum(p.astype(F32) for p in scatter([dwkv[j] for j in range(n)], DEC)).astype(BF)
    cross_total = jnp.where(decoder, dwx, to_encoder(dwkv))
    cross_total = lax.psum(cross_total, "dp").astype(F32)

    first_total, second_total = expert_grads(u_rows, dr_rows, first_weight, second_weight)

    self_total = self_total.reshape(width, 4, hl, hs).transpose(0, 2, 1, 3)
    cross_total = cross_total.reshape(width, 2, hl, hs).transpose(0, 2, 1, 3)
    return (
        jnp.stack(outs)[None],
        jnp.stack(input_grads)[None],
        self_total.reshape(1, width, hl, 4 * hs),
        cross_total.reshape(1, width, hl, 2 * hs),
        gain_total[None],
        first_total[None],
        second_total[None],
    )


def solution(mesh):
    rows = P("section", None, ("dp", "mp"), None)
    heads = P("section", None, "mp", None)
    expert = P("section", "mp", None, None)
    return jax.shard_map(
        on_device,
        mesh=mesh,
        in_specs=(rows, rows, rows, heads, heads, P("section", None, None), expert, expert),
        out_specs=(rows, rows, heads, heads, P("section", None, None), expert, expert),
        check_vma=False,
    )
```

time: 1540 us -> 709 us (0.46)
  waiting for transfers between devices: 857 us -> 307 us
  matrix products: 270 us -> 0 us
  Pallas kernels: 0 us -> 170 us
  blocking collectives: 95.7 us -> 0 us
  other arithmetic: 111 us -> 25.4 us
  local copies, waits for them, and re-layouts: 113 us -> 68.2 us
  starting transfers between devices: 68.1 us -> 110 us
    reduce_scatter x20 -> x0, waiting for transfers between devices: 359 us -> none  [spread(): lax.psum_scatter(partial_sum.astype(jnp.bfloat16), 'mp', scatter_dimensio...]
    psum x1, waiting for transfers between devices: 281 us -> 5.2 us  [on_device(): self_total = lax.psum(self_total, 'dp').astype(F32)]
    dot_general x63 -> x0, matrix products: 213 us -> none  [the longest x4 28.8 us: on_device(): jnp.einsum('secd,secf->edf', backward_kept['incoming'], before_grad, pref...]
    pallas_call x0 -> x30, Pallas kernels: none -> 170 us  [the longest x23 91.5 us: call(): pl.pallas_call(body, out_shape=shapes, in_specs=[SM] + [VM] * len(ins), o...]
    ppermute x6 -> x100, starting transfers between devices: 14.7 us -> 110 us  [the longest x90 95.9 us: swap(): return lax.ppermute(x, ('section', 'mp'), pairs)]
    ppermute x6 -> x100, waiting for transfers between devices: 74.3 us -> 155 us  [the longest x3 110 us: to_encoder(): return lax.ppermute(x, 'section', [(1, 0)])]
    all_gather x16 -> x4, waiting for transfers between devices: 80.7 us -> 147 us  [rows_of(): return lax.all_gather(whole, 'dp', axis=0, tiled=True)]
    all_to_all x6 -> x0, blocking collectives: 60.8 us -> none  [route(): return lax.all_to_all(buffer, 'mp', split_axis=0, concat_axis=0, tiled=True)]
  transfers between devices with their start and end apart: 57 -> 105, of which waited for: 40 -> 21; matrix products, arithmetic and copies ran while one was open for 22% -> 6% of each run, Pallas kernels for 0% -> 16%
where the time goes in v1:
time: 709 us; the launch traced here: 698 us
  waiting for transfers between devices  307 us (43%)
  Pallas kernels  170 us (24%)
  starting transfers between devices  110 us (16%)
  local copies, waits for them, and re-layouts  68.2 us (10%)
  other arithmetic  25.4 us (4%)
  between operations  16.3 us (2%)
    all_gather x4, waiting for transfers between devices, rows_of(): return lax.all_gather(whole, 'dp', axis=0, tiled=True)  147 us
    ppermute x3, waiting for transfers between devices, to_encoder(): return lax.ppermute(x, 'section', [(1, 0)])  110 us
    ppermute x90, starting transfers between devices, swap(): return lax.ppermute(x, ('section', 'mp'), pairs)  95.9 us
    pallas_call x23, Pallas kernels, call(): pl.pallas_call(body, out_shape=shapes, in_specs=[SM] + [VM] * len(ins), o...  91.5 us
    unnamed x307, local copies, waits for them, and re-layouts  55.7 us
    pallas_call x1, Pallas kernels, expert_grads(): pl.pallas_call(functools.partial(expert_grad_body, micro, chunk), grid=(e...  41.2 us
    ppermute x90, waiting for transfers between devices, swap(): return lax.ppermute(x, ('section', 'mp'), pairs)  41.1 us
    pallas_call x6, Pallas kernels, experts(): pl.pallas_call(functools.partial(expert_body, n, el, capp, steps, active,...  37.6 us
  transfers between devices with their start and end apart: 105, of which 21 were waited for; matrix products, arithmetic and copies ran while one was open for 6% of the time, Pallas kernels for 16%

profile of v1, /device:TPU:0, one launch (start us, length us, event | category | flops | bytes accessed | tf_op | source)
XLA Modules:
  0.0 697.7 jit_solution(4900930503839242040)
XLA Ops:
  8.3 3.0 collective-permute-start.1
  11.8 6.6 collective-permute-done.1.refs_2_
  20.1 3.1 collective-permute-done.30.refs_2_
  23.3 7.9 %shard_map.135 = (bf16[1024,512]{1,0:T(8,128)(2,1)S(1)}, bf16[1024,384]{1,0:T(8,128)(2,1)S(1)}, bf16[1024,128]{1,0:T(8,128)(2,1)S(1)}, f32[1024,128]{1,0:T(8,128...) custom-call(s32[2]{0:T(128)S(1)} %pad_add_fusion.scal, ...), custom_call_target="tpu_custom_call" | custom-call | flops 2684354560 | bytes 5244928 | tf_op jit(solution)/shard_map/pallas_call | solution.py:95
  36.5 8.2 %shard_map.143 = (bf16[1024,512]{1,0:T(8,128)(2,1)S(1)}, bf16[1024,384]{1,0:T(8,128)(2,1)S(1)}, bf16[1024,128]{1,0:T(8,128)(2,1)S(1)}, f32[1024,128]{1,0:T(8,128...) custom-call(s32[2]{0:T(128)S(1)} %pad_add_fusion.scal, ...), custom_call_target="tpu_custom_call" | custom-call | flops 2684354560 | bytes 5244928 | tf_op jit(solution)/shard_map/pallas_call | solution.py:95
  48.6 6.3 collective-permute-done.5.refs_3_
  63.2 8.5 %shard_map.138 = (bf16[96,512]{1,0:T(8,128)(2,1)S(1)}, bf16[96,512]{1,0:T(8,128)(2,1)}, bf16[96,512]{1,0:T(8,128)(2,1)S(1)}, bf16[96,512]{1,0:T(8,128)(2,1)S(1)}) custom-call(s32[2]{0:T(128)S(1)} %pad_add_fusion.scal, bf16[96,512]{1,0:T(8,128)(2,1)S(1)} %get-tuple-element.153.refs_0_.refs_4_, bf16[96,512]{1,0:T(8,128)(2,1)S(1)} %collective-permute-done.6.refs_1_.refs_5_, ...), custom_call_target="tpu_custom_call" | custom-call | flops 1610612736 | bytes 8388608 | tf_op jit(solution)/shard_map/pallas_call | solution.py:491
  72.3 2.4 collective-permute-start.9
  74.7 3.7 collective-permute-start.10
  97.7 2.2 copy-done.1
  99.9 7.8 %shard_map.145 = (bf16[96,512]{1,0:T(8,128)(2,1)S(1)}, bf16[96,512]{1,0:T(8,128)(2,1)S(1)}, bf16[96,512]{1,0:T(8,128)(2,1)S(1)}, bf16[96,512]{1,0:T(8,128)(2,1)S(1)}) custom-call(s32[2]{0:T(128)S(1)} %pad_add_fusion.scal, bf16[96,512]{1,0:T(8,128)(2,1)S(1)} %get-tuple-element.177.refs_0_.refs_4_, ...), custom_call_target="tpu_custom_call" | custom-call | flops 1610612736 | bytes 8388608 | tf_op jit(solution)/shard_map/pallas_call | solution.py:491
  109.7 3.7 collective-permute-start.39
  117.4 2.9 collective-permute-done.40.refs_3_
  125.5 3.2 collective-permute-done.41.refs_0_
  132.2 3.2 shard_map.140
  139.0 3.6 shard_map.147
  151.2 2.3 shard_map.148
  156.3 3.5 shard_map.150
  167.6 3.6 shard_map.157
  180.6 3.8 shard_map.153
  188.5 3.9 shard_map.160
  192.4 2.6 add_convert_fusion.1
  206.7 110.5 %collective-permute-done.57.refs_0_ = bf16[256,512]{1,0:T(8,128)(2,1)S(1)} collective-permute-done((bf16[256,512]{1,0:T(8,128)(2,1)S(1)}, bf16[256,512]{1,0:T(8,128)(2,1)S(1)}, u32[]{:S(2)}, u32[]{:S(2)}) %collective-permute-start.57) | collective-permute-done | bytes 262176 | tf_op jit(solution)/shard_map/ppermute | solution.py:620
  320.3 2.6 collective-permute-start.59
  323.0 3.1 collective-permute-start.60
  328.1 2.2 collective-permute-start.77
  330.3 2.6 collective-permute-start.78
  333.0 2.8 collective-permute-start.79
  335.7 8.6 %shard_map.152 = (bf16[96,512]{1,0:T(8,128)(2,1)S(1)}, bf16[96,512]{1,0:T(8,128)(2,1)S(1)}, bf16[96,512]{1,0:T(8,128)(2,1)S(1)}, bf16[96,512]{1,0:T(8,128)(2,1)S(1)}) custom-call(s32[2]{0:T(128)S(1)} %pad_add_fusion.scal, bf16[96,512]{1,0:T(8,128)(2,1)S(1)} %get-tuple-element.153.refs_0_.refs_4_, bf16[96,512]{1,0:T(8,128)(2,1)S(1)} %copy-done.4, ...), custom_call_target="tpu_custom_call" | custom-call | flops 2415919104 | bytes 8388608 | tf_op jit(solution)/shard_map/pallas_call | solution.py:491
  344.5 2.5 collective-permute-start.61
  347.0 2.6 collective-permute-start.62
  349.6 2.6 collective-permute-start.63
  352.2 8.6 %shard_map.159 = (bf16[96,512]{1,0:T(8,128)(2,1)S(1)}, bf16[96,512]{1,0:T(8,128)(2,1)S(1)}, bf16[96,512]{1,0:T(8,128)(2,1)S(1)}, bf16[96,512]{1,0:T(8,128)(2,1)S(1)}) custom-call(s32[2]{0:T(128)S(1)} %pad_add_fusion.scal, bf16[96,512]{1,0:T(8,128)(2,1)S(1)} %get-tuple-element.177.refs_0_.refs_4_, ...), custom_call_target="tpu_custom_call" | custom-call | flops 2415919104 | bytes 8388608 | tf_op jit(solution)/shard_map/pallas_call | solution.py:491
  363.0 2.7 collective-permute-start.80
  370.3 3.2 collective-permute-start.81
  373.6 4.5 collective-permute-done.81.refs_2_
  380.0 4.5 collective-permute-done.82.refs_3_
  400.0 18.6 %shard_map.155 = (bf16[256,512]{1,0:T(8,128)(2,1)S(1)}, bf16[256,512]{1,0:T(8,128)(2,1)S(1)}, bf16[256,512]{1,0:T(8,128)(2,1)S(1)}, bf16[256,512]{1,0:T(8,128)(2...) custom-call(s32[2]{0:T(128)S(1)} %pad_add_fusion.scal, bf16[256,512]{1,0:T(8,128)(2,1)} %get-tuple-element.225.refs_0_, ...), custom_call_target="tpu_custom_call" | custom-call | flops 6442450944 | bytes 6295552 | tf_op jit(solution)/shard_map/pallas_call | solution.py:95
  420.8 20.4 %shard_map.162 = (bf16[256,512]{1,0:T(8,128)(2,1)S(1)}, bf16[256,512]{1,0:T(8,128)(2,1)S(1)}, bf16[256,512]{1,0:T(8,128)(2,1)S(1)}, bf16[256,512]{1,0:T(8,128)(2...) custom-call(s32[2]{0:T(128)S(1)} %pad_add_fusion.scal, bf16[256,512]{1,0:T(8,128)(2,1)} %get-tuple-element.263.refs_0_, ...), custom_call_target="tpu_custom_call" | custom-call | flops 6442450944 | bytes 6295552 | tf_op jit(solution)/shard_map/pallas_call | solution.py:95
  470.8 2.7 collective-permute-start.99
  477.3 5.6 collective-permute-done.69.refs_2_
  483.8 3.5 collective-permute-done.88.refs_2_
  489.3 5.2 all-reduce.3.cloned.1.call-done
  498.4 34.7 %all-gather.5.cloned.1.call-done.refs_0_ = bf16[16,2,48,512]{3,2,1,0:T(8,128)(2,1)} async-done(((bf16[4,2,48,512]{3,2,1,0:T(8,128)(2,1)}), bf16[16,2,48,512]{3,2,1,0:T(8,128)(2,1)}) %all-gather.5.cloned.1.call-update) | async-done | bytes 1572880 | tf_op jit(solution)/shard_map/all_gather | solution.py:780
  533.1 37.6 %all-gather.9.cloned.1.call-done.refs_2_ = bf16[16,2,48,512]{3,2,1,0:T(8,128)(2,1)} async-done(((bf16[4,2,48,512]{3,2,1,0:T(8,128)(2,1)}), bf16[16,2,48,512]{3,2,1,0:T(8,128)(2,1)}) %all-gather.9.cloned.1.call-update) | async-done | bytes 1572880 | tf_op jit(solution)/shard_map/all_gather | solution.py:780
  570.7 37.4 %all-gather.7.cloned.1.call-done.refs_1_ = bf16[16,2,48,512]{3,2,1,0:T(8,128)(2,1)} async-done(((bf16[4,2,48,512]{3,2,1,0:T(8,128)(2,1)}), bf16[16,2,48,512]{3,2,1,0:T(8,128)(2,1)}) %all-gather.7.cloned.1.call-update) | async-done | bytes 1572880 | tf_op jit(solution)/shard_map/all_gather | solution.py:780
  608.1 37.4 %all-gather.11.cloned.1.call-done.refs_3_ = bf16[16,2,48,512]{3,2,1,0:T(8,128)(2,1)} async-done(((bf16[4,2,48,512]{3,2,1,0:T(8,128)(2,1)}), bf16[16,2,48,512]{3,2,1,0:T(8,128)(2,1)}) %all-gather.11.cloned.1.call-update) | async-done | bytes 1572880 | tf_op jit(solution)/shard_map/all_gather | solution.py:780
  649.7 41.2 %shard_map.164 = (f32[2,512,2048]{2,1,0:T(8,128)}, f32[2,2048,512]{2,1,0:T(8,128)}) custom-call(bf16[16,2,48,512]{3,2,1,0:T(8,128)(2,1)S(1)} %copy-done.83, bf16[16,2,48,512]{3,2,1,0:T(8,128)(2,1)S(1)} %copy-done.85, bf16[16,2,48,512]{3,2,1,0:T(8,128)(2,1)S(1)} %copy-done.84, bf16[16,2,48,512]{3,2,1,0:T(8,128)(2,1)} %all-gather.11.cloned.1.call-done.refs_3_, ...), custom_call_target="tpu_custom_call" | custom-call | flops 25769803776 | bytes 25165824 | tf_op jit(solution)/shard_map/pallas_call | solution.py:553
  (556 shorter events, 177.5 us)
Async XLA Ops:
  7.2 487.3 %all-reduce.3.cloned.1.call-start = ((), (), s32[]{:S(2)}) async-start(), calls=%async_computation.4 | async-start | bytes 1572864 | tf_op jit(solution)/shard_map/psum | solution.py:832
  8.3 10.2 %collective-permute-start.1 = (bf16[256,512]{1,0:T(8,128)(2,1)S(1)}, bf16[256,512]{1,0:T(8,128)(2,1)S(1)}, u32[]{:S(2)}, u32[]{:S(2)}) collective-permute-start(bf16[256,512]{1,0:T(8,128)(2,1)S(1)} %get-tuple-element.320.refs_0_.refs_4_), channel_id=1, source_target_pairs={{0,2},{1,3},{2,0},{3,1},{16,18},{17,19},{18,16},{19,17},{4,6},{5,7... | collective-permute-start | bytes 786440 | tf_op jit(solution)/shard_map/ppermute | solution.py:590
  11.3 11.9 %collective-permute-start = (bf16[256,512]{1,0:T(8,128)(2,1)S(1)}, bf16[256,512]{1,0:T(8,128)(2,1)S(1)}, u32[]{:S(2)}, u32[]{:S(2)}) collective-permute-start(bf16[256,512]{1,0:T(8,128)(2,1)S(1)} %get-tuple-element.320.refs_0_.refs_4_), channel_id=1, source_target_pairs={{0,1},{1,0},{2,3},{3,2},{16,17},{17,16},{18,19},{19,18},{4,5},{5,4... | collective-permute-start | bytes 786440 | tf_op jit(solution)/shard_map/ppermute | solution.py:590
  11.3 11.9 %collective-permute-start.30 = (bf16[256,512]{1,0:T(8,128)(2,1)S(1)}, bf16[256,512]{1,0:T(8,128)(2,1)S(1)}, u32[]{:S(2)}, u32[]{:S(2)}) collective-permute-start(bf16[256,512]{1,0:T(8,128)(2,1)S(1)} %get-tuple-element.321.refs_0_.refs_4_), channel_id=1, source_target_pairs={{0,2},{1,3},{2,0},{3,1},{16,18},{17,19},{18,16},{19,17},{4,6},{5,7... | collective-permute-start | bytes 786440 | tf_op jit(solution)/shard_map/ppermute | solution.py:590
  11.5 25.0 %collective-permute-start.29 = (bf16[256,512]{1,0:T(8,128)(2,1)S(1)}, bf16[256,512]{1,0:T(8,128)(2,1)S(1)}, u32[]{:S(2)}, u32[]{:S(2)}) collective-permute-start(bf16[256,512]{1,0:T(8,128)(2,1)S(1)} %get-tuple-element.321.refs_0_.refs_4_), channel_id=1, source_target_pairs={{0,1},{1,0},{2,3},{3,2},{16,17},{17,16},{18,19},{19,18},{4,5},{5,4... | collective-permute-start | bytes 786440 | tf_op jit(solution)/shard_map/ppermute | solution.py:590
  23.2 13.2 %collective-permute-start.31 = (bf16[256,512]{1,0:T(8,128)(2,1)S(1)}, bf16[256,512]{1,0:T(8,128)(2,1)}, u32[]{:S(2)}, u32[]{:S(2)}) collective-permute-start(bf16[256,512]{1,0:T(8,128)(2,1)S(1)} %collective-permute-done.30.refs_2_), channel_id=1, source_target_pairs={{0,1},{1,0},{2,3},{3,2},{16,17},{17,16},{18,19},{19,18},{4,5},{5,4... | collective-permute-start | bytes 786440 | tf_op jit(solution)/shard_map/ppermute | solution.py:590
  34.5 10.8 %collective-permute-start.4 = (bf16[256,512]{1,0:T(8,128)(2,1)}, bf16[256,512]{1,0:T(8,128)(2,1)}, u32[]{:S(2)}, u32[]{:S(2)}) collective-permute-start(bf16[256,512]{1,0:T(8,128)(2,1)} %get-tuple-element.152), channel_id=1, source_target_pairs={{0,1},{1,0},{2,3},{3,2},{16,17},{17,16},{18,19},{19,18},{4,5},{5,4... | collective-permute-start | bytes 786440 | tf_op jit(solution)/shard_map/ppermute | solution.py:590
  44.7 13.3 %collective-permute-start.33 = (bf16[256,512]{1,0:T(8,128)(2,1)S(1)}, bf16[256,512]{1,0:T(8,128)(2,1)S(1)}, u32[]{:S(2)}, u32[]{:S(2)}) collective-permute-start(bf16[256,512]{1,0:T(8,128)(2,1)S(1)} %get-tuple-element.176), channel_id=1, source_target_pairs={{0,1},{1,0},{2,3},{3,2},{16,17},{17,16},{18,19},{19,18},{4,5},{5,4... | collective-permute-start | bytes 786440 | tf_op jit(solution)/shard_map/ppermute | solution.py:590
  48.5 36.5 %collective-permute-start.32 = (bf16[256,512]{1,0:T(8,128)(2,1)}, bf16[256,512]{1,0:T(8,128)(2,1)S(1)}, u32[]{:S(2)}, u32[]{:S(2)}) collective-permute-start(bf16[256,512]{1,0:T(8,128)(2,1)} %get-tuple-element.174), channel_id=1, source_target_pairs={{0,1},{1,0},{2,3},{3,2},{16,17},{17,16},{18,19},{19,18},{4,5},{5,4... | collective-permute-start | bytes 786440 | tf_op jit(solution)/shard_map/ppermute | solution.py:590
  58.8 28.1 %collective-permute-start.34 = (bf16[256,512]{1,0:T(8,128)(2,1)}, bf16[256,512]{1,0:T(8,128)(2,1)S(1)}, u32[]{:S(2)}, u32[]{:S(2)}) collective-permute-start(bf16[256,512]{1,0:T(8,128)(2,1)} %add_convert_fusion.9), channel_id=1, source_target_pairs={{0,2},{1,3},{2,0},{3,1},{16,18},{17,19},{18,16},{19,17},{4,6},{5,7... | collective-permute-start | bytes 786440 | tf_op jit(solution)/shard_map/ppermute | solution.py:590
  72.3 16.2 %collective-permute-start.9 = (bf16[96,512]{1,0:T(8,128)(2,1)}, bf16[96,512]{1,0:T(8,128)(2,1)S(1)}, u32[]{:S(2)}, u32[]{:S(2)}) collective-permute-start(bf16[96,512]{1,0:T(8,128)(2,1)} %get-tuple-element.158), channel_id=1, source_target_pairs={{0,1},{1,0},{2,3},{3,2},{4,5},{5,4},{6,7},{7,6},{8,9},{9,8},{10,11... | collective-permute-start | bytes 294920 | tf_op jit(solution)/shard_map/ppermute | solution.py:590
  74.7 16.2 %collective-permute-start.10 = (bf16[96,512]{1,0:T(8,128)(2,1)S(1)}, bf16[96,512]{1,0:T(8,128)(2,1)S(1)}, u32[]{:S(2)}, u32[]{:S(2)}) collective-permute-start(bf16[96,512]{1,0:T(8,128)(2,1)S(1)} %get-tuple-element.159), channel_id=1, source_target_pairs={{0,2},{1,3},{2,0},{3,1},{4,6},{5,7},{6,4},{7,5},{8,10},{9,11},{10,... | collective-permute-start | bytes 294920 | tf_op jit(solution)/shard_map/ppermute | solution.py:590
  83.7 29.7 %collective-permute-start.19 = (bf16[512,256]{1,0:T(8,128)(2,1)}, bf16[512,256]{1,0:T(8,128)(2,1)S(1)}, u32[]{:S(2)}, u32[]{:S(2)}) collective-permute-start(bf16[512,256]{1,0:T(8,128)(2,1)} %copy.54.refs_4_.refs_0_), channel_id=1, source_target_pairs={{0,16},{1,17},{2,18},{3,19},{4,20},{5,21},{6,22},{7,23},{8,24},{9,... | collective-permute-start | bytes 786440 | tf_op jit(solution)/shard_map/ppermute | solution.py:617
  91.9 30.7 %collective-permute-start.17 = (bf16[512,256]{1,0:T(8,128)(2,1)}, bf16[512,256]{1,0:T(8,128)(2,1)S(1)}, u32[]{:S(2)}, u32[]{:S(2)}) collective-permute-start(bf16[512,256]{1,0:T(8,128)(2,1)} %copy.54.refs_4_.refs_0_), channel_id=1, source_target_pairs={{16,18},{17,19},{18,16},{19,17},{20,22},{21,23},{22,20},{23,21},{2... | collective-permute-start | bytes 786440 | tf_op jit(solution)/shard_map/ppermute | solution.py:590
  96.4 27.0 %collective-permute-start.12 = (bf16[256,512]{1,0:T(8,128)(2,1)S(1)}, bf16[256,512]{1,0:T(8,128)(2,1)S(1)}, u32[]{:S(2)}, u32[]{:S(2)}) collective-permute-start(bf16[256,512]{1,0:T(8,128)(2,1)S(1)} %get-tuple-element.162), channel_id=1, source_target_pairs={{0,16},{1,17},{2,18},{3,19},{4,20},{5,21},{6,22},{7,23},{8,24},{9,... | collective-permute-start | bytes 786440 | tf_op jit(solution)/shard_map/ppermute | solution.py:617
  154.2 10.6 %collective-permute-start.70 = (bf16[96,512]{1,0:T(8,128)(2,1)S(1)}, bf16[96,512]{1,0:T(8,128)(2,1)S(1)}, u32[]{:S(2)}, u32[]{:S(2)}) collective-permute-start(bf16[96,512]{1,0:T(8,128)(2,1)S(1)} %get-tuple-element.236), channel_id=1, source_target_pairs={{16,17},{17,16},{18,19},{19,18},{20,21},{21,20},{22,23},{23,22},{2... | collective-permute-start | bytes 294920 | tf_op jit(solution)/shard_map/ppermute | solution.py:590
  154.9 9.9 %collective-permute-start.71 = (bf16[96,512]{1,0:T(8,128)(2,1)S(1)}, bf16[96,512]{1,0:T(8,128)(2,1)S(1)}, u32[]{:S(2)}, u32[]{:S(2)}) collective-permute-start(bf16[96,512]{1,0:T(8,128)(2,1)S(1)} %get-tuple-element.237), channel_id=1, source_target_pairs={{16,18},{17,19},{18,16},{19,17},{20,22},{21,23},{22,20},{23,21},{2... | collective-permute-start | bytes 294920 | tf_op jit(solution)/shard_map/ppermute | solution.py:590
  162.0 37.7 %collective-permute-start.54 = (bf16[256,512]{1,0:T(8,128)(2,1)S(1)}, bf16[256,512]{1,0:T(8,128)(2,1)}, u32[]{:S(2)}, u32[]{:S(2)}) collective-permute-start(bf16[256,512]{1,0:T(8,128)(2,1)S(1)} %get-tuple-element.206), channel_id=1, source_target_pairs={{16,17},{17,16},{18,19},{19,18},{20,21},{21,20},{22,23},{23,22},{2... | collective-permute-start | bytes 786440 | tf_op jit(solution)/shard_map/ppermute | solution.py:590
  163.4 32.9 %collective-permute-start.55 = (bf16[256,512]{1,0:T(8,128)(2,1)S(1)}, bf16[256,512]{1,0:T(8,128)(2,1)}, u32[]{:S(2)}, u32[]{:S(2)}) collective-permute-start(bf16[256,512]{1,0:T(8,128)(2,1)S(1)} %get-tuple-element.208), channel_id=1, source_target_pairs={{16,17},{17,16},{18,19},{19,18},{20,21},{21,20},{22,23},{23,22},{2... | collective-permute-start | bytes 786440 | tf_op jit(solution)/shard_map/ppermute | solution.py:590
  172.8 29.4 %collective-permute-start.73 = (bf16[256,512]{1,0:T(8,128)(2,1)S(1)}, bf16[256,512]{1,0:T(8,128)(2,1)}, u32[]{:S(2)}, u32[]{:S(2)}) collective-permute-start(bf16[256,512]{1,0:T(8,128)(2,1)S(1)} %get-tuple-element.244), channel_id=1, source_target_pairs={{16,17},{17,16},{18,19},{19,18},{20,21},{21,20},{22,23},{23,22},{2... | collective-permute-start | bytes 786440 | tf_op jit(solution)/shard_map/ppermute | solution.py:590
  174.1 23.9 %collective-permute-start.74 = (bf16[256,512]{1,0:T(8,128)(2,1)S(1)}, bf16[256,512]{1,0:T(8,128)(2,1)}, u32[]{:S(2)}, u32[]{:S(2)}) collective-permute-start(bf16[256,512]{1,0:T(8,128)(2,1)S(1)} %get-tuple-element.246), channel_id=1, source_target_pairs={{16,17},{17,16},{18,19},{19,18},{20,21},{21,20},{22,23},{23,22},{2... | collective-permute-start | bytes 786440 | tf_op jit(solution)/shard_map/ppermute | solution.py:590
  195.0 10.8 %collective-permute-start.90 = (bf16[512,256]{1,0:T(8,128)(2,1)S(1)}, bf16[512,256]{1,0:T(8,128)(2,1)S(1)}, u32[]{:S(2)}, u32[]{:S(2)}) collective-permute-start(bf16[512,256]{1,0:T(8,128)(2,1)S(1)} %get-tuple-element.315), channel_id=1, source_target_pairs={{16,17},{17,16},{18,19},{19,18},{20,21},{21,20},{22,23},{23,22},{2... | collective-permute-start | bytes 786440 | tf_op jit(solution)/shard_map/ppermute | solution.py:590
  199.7 167.7 %collective-permute-start.92 = (bf16[512,256]{1,0:T(8,128)(2,1)S(1)}, bf16[512,256]{1,0:T(8,128)(2,1)S(1)}, u32[]{:S(2)}, u32[]{:S(2)}) collective-permute-start(bf16[512,256]{1,0:T(8,128)(2,1)S(1)} %get-tuple-element.316), channel_id=1, source_target_pairs={{16,17},{17,16},{18,19},{19,18},{20,21},{21,20},{22,23},{23,22},{2... | collective-permute-start | bytes 786440 | tf_op jit(solution)/shard_map/ppermute | solution.py:590
  200.4 122.5 %collective-permute-start.93 = (bf16[512,256]{1,0:T(8,128)(2,1)S(1)}, bf16[512,256]{1,0:T(8,128)(2,1)S(1)}, u32[]{:S(2)}, u32[]{:S(2)}) collective-permute-start(bf16[512,256]{1,0:T(8,128)(2,1)S(1)} %get-tuple-element.317), channel_id=1, source_target_pairs={{16,17},{17,16},{18,19},{19,18},{20,21},{21,20},{22,23},{23,22},{2... | collective-permute-start | bytes 786440 | tf_op jit(solution)/shard_map/ppermute | solution.py:590
  202.2 115.0 %collective-permute-start.57 = (bf16[256,512]{1,0:T(8,128)(2,1)S(1)}, bf16[256,512]{1,0:T(8,128)(2,1)S(1)}, u32[]{:S(2)}, u32[]{:S(2)}) collective-permute-start(bf16[256,512]{1,0:T(8,128)(2,1)S(1)} %add_convert_fusion.7), channel_id=1, source_target_pairs={{16,0},{17,1},{18,2},{19,3},{20,4},{21,5},{22,6},{23,7},{24,8},{25... | collective-permute-start | bytes 786440 | tf_op jit(solution)/shard_map/ppermute | solution.py:620
  204.6 121.6 %collective-permute-start.76 = (bf16[256,512]{1,0:T(8,128)(2,1)S(1)}, bf16[256,512]{1,0:T(8,128)(2,1)S(1)}, u32[]{:S(2)}, u32[]{:S(2)}) collective-permute-start(bf16[256,512]{1,0:T(8,128)(2,1)S(1)} %add_convert_fusion.4), channel_id=1, source_target_pairs={{16,0},{17,1},{18,2},{19,3},{20,4},{21,5},{22,6},{23,7},{24,8},{25... | collective-permute-start | bytes 786440 | tf_op jit(solution)/shard_map/ppermute | solution.py:620
  320.3 10.0 %collective-permute-start.59 = (bf16[96,512]{1,0:T(8,128)(2,1)S(1)}, bf16[96,512]{1,0:T(8,128)(2,1)S(1)}, u32[]{:S(2)}, u32[]{:S(2)}) collective-permute-start(bf16[96,512]{1,0:T(8,128)(2,1)S(1)} %get-tuple-element.211), channel_id=1, source_target_pairs={{0,2},{1,3},{2,0},{3,1},{4,6},{5,7},{6,4},{7,5},{8,10},{9,11},{10,... | collective-permute-start | bytes 294920 | tf_op jit(solution)/shard_map/ppermute | solution.py:590
  323.0 10.0 %collective-permute-start.60 = (bf16[96,512]{1,0:T(8,128)(2,1)S(1)}, bf16[96,512]{1,0:T(8,128)(2,1)S(1)}, u32[]{:S(2)}, u32[]{:S(2)}) collective-permute-start(bf16[96,512]{1,0:T(8,128)(2,1)S(1)} %get-tuple-element.212), channel_id=1, source_target_pairs={{0,3},{1,2},{2,1},{3,0},{4,7},{5,6},{6,5},{7,4},{8,11},{9,10},{10,... | collective-permute-start | bytes 294920 | tf_op jit(solution)/shard_map/ppermute | solution.py:590
  326.1 42.1 %collective-permute-start.94 = (bf16[512,256]{1,0:T(8,128)(2,1)S(1)}, bf16[512,256]{1,0:T(8,128)(2,1)S(1)}, u32[]{:S(2)}, u32[]{:S(2)}) collective-permute-start(bf16[512,256]{1,0:T(8,128)(2,1)S(1)} %fusion), channel_id=1, source_target_pairs={{16,18},{17,19},{18,16},{19,17},{20,22},{21,23},{22,20},{23,21},{2... | collective-permute-start | bytes 786440 | tf_op jit(solution)/shard_map/ppermute | solution.py:590
  328.1 16.4 %collective-permute-start.77 = (bf16[96,512]{1,0:T(8,128)(2,1)S(1)}, bf16[96,512]{1,0:T(8,128)(2,1)S(1)}, u32[]{:S(2)}, u32[]{:S(2)}) collective-permute-start(bf16[96,512]{1,0:T(8,128)(2,1)S(1)} %get-tuple-element.248), channel_id=1, source_target_pairs={{0,1},{1,0},{2,3},{3,2},{4,5},{5,4},{6,7},{7,6},{8,9},{9,8},{10,11... | collective-permute-start | bytes 294920 | tf_op jit(solution)/shard_map/ppermute | solution.py:590
  330.3 16.6 %collective-permute-start.78 = (bf16[96,512]{1,0:T(8,128)(2,1)S(1)}, bf16[96,512]{1,0:T(8,128)(2,1)S(1)}, u32[]{:S(2)}, u32[]{:S(2)}) collective-permute-start(bf16[96,512]{1,0:T(8,128)(2,1)S(1)} %get-tuple-element.249), channel_id=1, source_target_pairs={{0,2},{1,3},{2,0},{3,1},{4,6},{5,7},{6,4},{7,5},{8,10},{9,11},{10,... | collective-permute-start | bytes 294920 | tf_op jit(solution)/shard_map/ppermute | solution.py:590
  333.0 16.6 %collective-permute-start.79 = (bf16[96,512]{1,0:T(8,128)(2,1)S(1)}, bf16[96,512]{1,0:T(8,128)(2,1)S(1)}, u32[]{:S(2)}, u32[]{:S(2)}) collective-permute-start(bf16[96,512]{1,0:T(8,128)(2,1)S(1)} %get-tuple-element.250), channel_id=1, source_target_pairs={{0,3},{1,2},{2,1},{3,0},{4,7},{5,6},{6,5},{7,4},{8,11},{9,10},{10,... | collective-permute-start | bytes 294920 | tf_op jit(solution)/shard_map/ppermute | solution.py:590
  344.5 16.4 %collective-permute-start.61 = (bf16[96,512]{1,0:T(8,128)(2,1)S(1)}, bf16[96,512]{1,0:T(8,128)(2,1)S(1)}, u32[]{:S(2)}, u32[]{:S(2)}) collective-permute-start(bf16[96,512]{1,0:T(8,128)(2,1)S(1)} %get-tuple-element.214), channel_id=1, source_target_pairs={{0,1},{1,0},{2,3},{3,2},{4,5},{5,4},{6,7},{7,6},{8,9},{9,8},{10,11... | collective-permute-start | bytes 294920 | tf_op jit(solution)/shard_map/ppermute | solution.py:590
  347.0 14.6 %collective-permute-start.62 = (bf16[96,512]{1,0:T(8,128)(2,1)S(1)}, bf16[96,512]{1,0:T(8,128)(2,1)S(1)}, u32[]{:S(2)}, u32[]{:S(2)}) collective-permute-start(bf16[96,512]{1,0:T(8,128)(2,1)S(1)} %get-tuple-element.215), channel_id=1, source_target_pairs={{0,2},{1,3},{2,0},{3,1},{4,6},{5,7},{6,4},{7,5},{8,10},{9,11},{10,... | collective-permute-start | bytes 294920 | tf_op jit(solution)/shard_map/ppermute | solution.py:590
  349.6 13.4 %collective-permute-start.63 = (bf16[96,512]{1,0:T(8,128)(2,1)S(1)}, bf16[96,512]{1,0:T(8,128)(2,1)S(1)}, u32[]{:S(2)}, u32[]{:S(2)}) collective-permute-start(bf16[96,512]{1,0:T(8,128)(2,1)S(1)} %get-tuple-element.216), channel_id=1, source_target_pairs={{0,3},{1,2},{2,1},{3,0},{4,7},{5,6},{6,5},{7,4},{8,11},{9,10},{10,... | collective-permute-start | bytes 294920 | tf_op jit(solution)/shard_map/ppermute | solution.py:590
  360.9 27.3 %collective-permute-start.89 = (bf16[512,256]{1,0:T(8,128)(2,1)S(1)}, bf16[512,256]{1,0:T(8,128)(2,1)S(1)}, u32[]{:S(2)}, u32[]{:S(2)}) collective-permute-start(bf16[512,256]{1,0:T(8,128)(2,1)S(1)} %get-tuple-element.314), channel_id=1, source_target_pairs={{16,17},{17,16},{18,19},{19,18},{20,21},{21,20},{22,23},{23,22},{2... | collective-permute-start | bytes 786440 | tf_op jit(solution)/shard_map/ppermute | solution.py:590
  361.6 27.3 %collective-permute-start.91 = (bf16[512,256]{1,0:T(8,128)(2,1)}, bf16[512,256]{1,0:T(8,128)(2,1)}, u32[]{:S(2)}, u32[]{:S(2)}) collective-permute-start(bf16[512,256]{1,0:T(8,128)(2,1)} %fusion.3), channel_id=1, source_target_pairs={{16,18},{17,19},{18,16},{19,17},{20,22},{21,23},{22,20},{23,21},{2... | collective-permute-start | bytes 786440 | tf_op jit(solution)/shard_map/ppermute | solution.py:590
  367.5 20.8 %collective-permute-start.65 = (bf16[256,512]{1,0:T(8,128)(2,1)}, bf16[256,512]{1,0:T(8,128)(2,1)S(1)}, u32[]{:S(2)}, u32[]{:S(2)}) collective-permute-start(bf16[256,512]{1,0:T(8,128)(2,1)} %get-tuple-element.225.refs_0_), channel_id=1, source_target_pairs={{0,2},{1,3},{2,0},{3,1},{16,18},{17,19},{18,16},{19,17},{4,6},{5,7... | collective-permute-start | bytes 786440 | tf_op jit(solution)/shard_map/ppermute | solution.py:590
  369.0 19.9 %collective-permute-start.95 = (bf16[512,256]{1,0:T(8,128)(2,1)}, bf16[512,256]{1,0:T(8,128)(2,1)}, u32[]{:S(2)}, u32[]{:S(2)}) collective-permute-start(bf16[512,256]{1,0:T(8,128)(2,1)} %fusion.2), channel_id=1, source_target_pairs={{16,0},{17,1},{18,2},{19,3},{20,4},{21,5},{22,6},{23,7},{24,8},{25... | collective-permute-start | bytes 786440 | tf_op jit(solution)/shard_map/ppermute | solution.py:620
  394.4 26.4 %collective-permute-start.83 = (bf16[256,512]{1,0:T(8,128)(2,1)}, bf16[256,512]{1,0:T(8,128)(2,1)S(1)}, u32[]{:S(2)}, u32[]{:S(2)}) collective-permute-start(bf16[256,512]{1,0:T(8,128)(2,1)} %get-tuple-element.263.refs_0_), channel_id=1, source_target_pairs={{0,1},{1,0},{2,3},{3,2},{16,17},{17,16},{18,19},{19,18},{4,5},{5,4... | collective-permute-start | bytes 786440 | tf_op jit(solution)/shard_map/ppermute | solution.py:590
  395.2 25.6 %collective-permute-start.85 = (bf16[256,512]{1,0:T(8,128)(2,1)}, bf16[256,512]{1,0:T(8,128)(2,1)S(1)}, u32[]{:S(2)}, u32[]{:S(2)}) collective-permute-start(bf16[256,512]{1,0:T(8,128)(2,1)} %collective-permute-done.84.refs_2_), channel_id=1, source_target_pairs={{0,1},{1,0},{2,3},{3,2},{16,17},{17,16},{18,19},{19,18},{4,5},{5,4... | collective-permute-start | bytes 786440 | tf_op jit(solution)/shard_map/ppermute | solution.py:590
  449.7 83.4 %all-gather.5.cloned.1.call-start = ((), (), s32[]{:S(2)}) async-start(), calls=%async_computation | async-start | bytes 1966080 | tf_op jit(solution)/shard_map/all_gather | solution.py:780
  452.6 118.0 %all-gather.9.cloned.1.call-start = ((), (), s32[]{:S(2)}) async-start(), calls=%async_computation.2 | async-start | bytes 1966080 | tf_op jit(solution)/shard_map/all_gather | solution.py:780
  454.6 153.4 %all-gather.7.cloned.1.call-start = ((), (), s32[]{:S(2)}) async-start(), calls=%async_computation.1 | async-start | bytes 1966080 | tf_op jit(solution)/shard_map/all_gather | solution.py:780
  457.6 187.9 %all-gather.11.cloned.1.call-start = ((), (), s32[]{:S(2)}) async-start(), calls=%async_computation.3 | async-start | bytes 1966080 | tf_op jit(solution)/shard_map/all_gather | solution.py:780
  462.2 11.3 %collective-permute-start.68 = (bf16[256,512]{1,0:T(8,128)(2,1)}, bf16[256,512]{1,0:T(8,128)(2,1)S(1)}, u32[]{:S(2)}, u32[]{:S(2)}) collective-permute-start(bf16[256,512]{1,0:T(8,128)(2,1)} %copy-done.92), channel_id=1, source_target_pairs={{0,1},{1,0},{2,3},{3,2},{16,17},{17,16},{18,19},{19,18},{4,5},{5,4... | collective-permute-start | bytes 786440 | tf_op jit(solution)/shard_map/ppermute | solution.py:590
  470.3 13.5 %collective-permute-start.86 = (bf16[256,512]{1,0:T(8,128)(2,1)S(1)}, bf16[256,512]{1,0:T(8,128)(2,1)S(1)}, u32[]{:S(2)}, u32[]{:S(2)}) collective-permute-start(bf16[256,512]{1,0:T(8,128)(2,1)S(1)} %copy-done.89), channel_id=1, source_target_pairs={{0,1},{1,0},{2,3},{3,2},{16,17},{17,16},{18,19},{19,18},{4,5},{5,4... | collective-permute-start | bytes 786440 | tf_op jit(solution)/shard_map/ppermute | solution.py:590
  475.1 12.2 %collective-permute-start.88 = (bf16[256,512]{1,0:T(8,128)(2,1)S(1)}, bf16[256,512]{1,0:T(8,128)(2,1)S(1)}, u32[]{:S(2)}, u32[]{:S(2)}) collective-permute-start(bf16[256,512]{1,0:T(8,128)(2,1)S(1)} %add_convert_fusion.3), channel_id=1, source_target_pairs={{0,2},{1,3},{2,0},{3,1},{16,18},{17,19},{18,16},{19,17},{4,6},{5,7... | collective-permute-start | bytes 786440 | tf_op jit(solution)/shard_map/ppermute | solution.py:590
  (208 other events, 1993.0 us)
Sparse Core Ops, SparseCore 0:
  449.8 44.6 all-reduce.2
  496.6 36.4 all-gather.4
  534.7 35.9 all-gather.8
  572.1 35.9 all-gather.6
  609.5 35.9 all-gather.10
